TPU v7x, 512 devices: a whole 4x8x8 slice. The times are simulated.
512 devices in a mesh: lat: 8 (over x, core), lon: 16 (over z_hi, y), fsdp: 4 (over z_lo).
Axes of the slice: x: 4, y: 8, z: 8 (z_hi: 2, z_lo: 4; z = z_hi * 4 + z_lo), core: 2. Of those that a mesh axis runs over, the one named last changes fastest.
Arguments:
- tokens: bfloat16 [64, 256, 1024], P('lat', 'lon'), may hold values from -8 to 8
- grad_out: bfloat16 [64, 256, 1024], P('lat', 'lon', 'fsdp'), may hold values from -6 to 6
- weight: bfloat16 [3, 1024, 1024], P(None, 'fsdp'), may hold values from -4 to 4
Outputs:
- grad_input: bfloat16 [64, 256, 1024], P('lat', 'lon', 'fsdp')
- grad_weight: float32 [3, 1024, 1024], P(None, ('lat', 'lon'), 'fsdp')
All inputs are finite; a program needn't handle non-finite values.
Results may differ from a plain program's by a relative error of at most 0.011.
The roundings to bfloat16 on the way count: a program that leaves them out, or rounds other values in their place, can miss the bound.
Values may be sent and summed in bfloat16 or wider, within the bound.
A program may use at most 64 MiB of HBM per device.

v0:
```python
import math

import jax
import jax.numpy as jnp
from jax import lax
from jax.sharding import PartitionSpec as P

HEADS = 16
RADIUS = 6


def extended_2(block, sides, width):
    for axis, dim in sides:
        count = lax.axis_size(axis)
        forward = [(i, i + 1) for i in range(count - 1)]
        forward.append((count - 1, 0))
        backward = [(target, source) for source, target in forward]
        low = lax.ppermute(
            lax.slice_in_dim(block, block.shape[dim] - width, None, axis=dim), axis, forward
        )
        high = lax.ppermute(lax.slice_in_dim(block, 0, width, axis=dim), axis, backward)
        block = jnp.concatenate([low, block, high], axis=dim)
    return block


def stack_band(extended_field, row_count, band_width):
    return jnp.stack([extended_field[offset : offset + row_count] for offset in range(band_width)])


def fold_band(band_terms, row_count):
    band_width = band_terms.shape[0]
    padding_rest = ((0, 0),) * (band_terms.ndim - 2)
    running = jnp.zeros((row_count + band_width - 1,) + band_terms.shape[2:], jnp.float32)
    for offset in range(band_width):
        running = running + jnp.pad(
            band_terms[offset], ((offset, band_width - 1 - offset),) + padding_rest
        )
    return running


def shards(tokens, grad_out, weight):
    lat_rows, lon_cols, model_width = tokens.shape
    own_cols = grad_out.shape[2]
    own_rows = weight.shape[1]
    head_size = model_width // HEADS
    local_heads = own_cols // head_size
    score_scale = 1.0 / math.sqrt(head_size)
    radius = RADIUS
    window_reach = 2 * radius + 1
    ext_cols = lon_cols + 2 * radius
    tok_count = lat_rows * lon_cols
    flat_tokens = tokens.reshape(tok_count, model_width)
    fsdp_index = lax.axis_index("fsdp")
    own_weight = lax.dynamic_slice_in_dim(
        lax.all_gather(weight, "fsdp", axis=1, tiled=True), fsdp_index * own_cols, own_cols, 2
    )
    projected = jnp.einsum(
        "td,cdk->tck", flat_tokens, own_weight, preferred_element_type=jnp.float32
    ).astype(jnp.bfloat16)
    queries = projected[:, 0].reshape(lat_rows, lon_cols, own_cols)
    pair_kv = projected[:, 1:].reshape(lat_rows, lon_cols, 2 * own_cols)
    extended = extended_2(pair_kv, (("lat", 0), ("lon", 1)), radius)
    band_row = jnp.arange(window_reach)[:, None] + jnp.arange(lat_rows)[None, :]
    global_row = lax.axis_index("lat") * lat_rows - radius + band_row
    lat_total = lat_rows * lax.axis_size("lat")
    lat_ok = (global_row >= 0) & (global_row < lat_total)
    col_gap = jnp.arange(ext_cols)[None, :] - jnp.arange(lon_cols)[:, None] - radius
    lon_ok = jnp.abs(col_gap) <= radius
    allowed = lat_ok[:, :, None, None] & lon_ok[None, None]
    query_parts = []
    key_grads = []
    value_grads = []
    for head_number in range(local_heads):
        head_cols = slice(head_number * head_size, (head_number + 1) * head_size)
        value_cols = slice(
            own_cols + head_number * head_size, own_cols + (head_number + 1) * head_size
        )
        head_query = queries[..., head_cols]
        head_grad = grad_out[..., head_cols]
        key_band = stack_band(extended[..., head_cols], lat_rows, window_reach)
        value_band = stack_band(extended[..., value_cols], lat_rows, window_reach)
        scores = score_scale * jnp.einsum(
            "rqd,arkd->arqk", head_query, key_band, preferred_element_type=jnp.float32
        )
        scores = jnp.where(allowed, scores, -jnp.inf)
        row_max = jnp.max(scores, axis=(0, 3))
        exp_scores = jnp.exp(scores - row_max[None, :, :, None])
        row_sum = jnp.sum(exp_scores, axis=(0, 3))
        attn_prob = exp_scores / row_sum[None, :, :, None]
        grad_prob = jnp.einsum(
            "rqd,arkd->arqk", head_grad, value_band, preferred_element_type=jnp.float32
        )
        delta_row = jnp.sum(attn_prob * grad_prob, axis=(0, 3))
        grad_score = (score_scale * (attn_prob * (grad_prob - delta_row[None, :, :, None]))).astype(
            jnp.bfloat16
        )
        query_parts.append(
            jnp.einsum("arqk,arkd->rqd", grad_score, key_band, preferred_element_type=jnp.float32)
        )
        prob_rounded = attn_prob.astype(jnp.bfloat16)
        key_grads.append(
            fold_band(
                jnp.einsum(
                    "arqk,rqd->arkd", grad_score, head_query, preferred_element_type=jnp.float32
                ),
                lat_rows,
            )
        )
        value_grads.append(
            fold_band(
                jnp.einsum(
                    "arqk,rqd->arkd", prob_rounded, head_grad, preferred_element_type=jnp.float32
                ),
                lat_rows,
            )
        )
    grad_query = jnp.concatenate(query_parts, 2)
    key_parts = jnp.concatenate(key_grads + value_grads, 2)
    returned = extended_2(key_parts.astype(jnp.bfloat16), (("lat", 0), ("lon", 1)), radius).astype(
        key_parts.dtype
    )
    inner_rows = slice(2 * radius, 2 * radius + lat_rows)
    inner_cols = slice(2 * radius, 2 * radius + lon_cols)
    far_rows = lat_rows + 3 * radius
    far_cols = lon_cols + 3 * radius
    summed = key_parts[radius : radius + lat_rows, radius : radius + lon_cols]
    summed = summed.at[:radius, :].add(returned[:radius, inner_cols])
    summed = summed.at[lat_rows - radius :, :].add(returned[far_rows:, inner_cols])
    summed = summed.at[:, :radius].add(returned[inner_rows, :radius])
    summed = summed.at[:, lon_cols - radius :].add(returned[inner_rows, far_cols:])
    summed = summed.at[:radius, :radius].add(returned[:radius, :radius])
    summed = summed.at[:radius, lon_cols - radius :].add(returned[:radius, far_cols:])
    summed = summed.at[lat_rows - radius :, :radius].add(returned[far_rows:, :radius])
    summed = summed.at[lat_rows - radius :, lon_cols - radius :].add(returned[far_rows:, far_cols:])
    grad_all = (
        jnp.stack([grad_query, summed[..., :own_cols], summed[..., own_cols:]], 2)
        .astype(jnp.bfloat16)
        .reshape(tok_count, 3, own_cols)
    )
    input_sum = jnp.einsum(
        "tcp,cdp->td",
        lax.all_gather(grad_all, "fsdp", axis=2, tiled=True),
        weight,
        preferred_element_type=jnp.float32,
    )
    grad_input = input_sum.astype(jnp.bfloat16).reshape(lat_rows, lon_cols, own_rows)
    token_total = tok_count * lax.axis_size("lat") * lax.axis_size("lon")
    weight_scale = 1.0 / math.sqrt(token_total)
    grad_weight = lax.psum_scatter(
        jnp.einsum("tr,tck->rck", flat_tokens, grad_all, preferred_element_type=jnp.float32)
        * weight_scale,
        ("lat", "lon"),
        scatter_dimension=0,
        tiled=True,
    )
    return (grad_input, jnp.transpose(grad_weight, (1, 0, 2)))


def solution(mesh):
    placed = (P("lat", "lon", None), P("lat", "lon", "fsdp"), P(None, "fsdp", None))
    return jax.shard_map(
        shards,
        mesh=mesh,
        in_specs=placed,
        out_specs=(P("lat", "lon", "fsdp"), P(None, ("lat", "lon"), "fsdp")),
        check_vma=False,
    )
```

profile of v0, /device:TPU:64, one launch (start us, length us, event | category | flops | bytes accessed | tf_op | source)
XLA Modules:
  0.0 1817.5 jit_solution(13528067327006108066)
XLA Ops:
  8.6 127.0 %all-gather.2.cloned.1.call-done = bf16[3,1024,1024]{2,1,0:T(8,128)(2,1)} async-done(((bf16[3,256,1024]{2,1,0:T(8,128)(2,1)}), bf16[3,1024,1024]{2,1,0:T(8,128)(2,1)}) %all-gather.2.cloned.1.call-update) | async-done | bytes 6291472 | tf_op jit(solution)/shard_map/all_gather | solution.py:55
  135.5 1.8 fusion.10
  138.0 2.9 collective-permute-start.1
  141.0 1.8 collective-permute-done
  143.2 3.4 collective-permute-start.2
  146.6 8.5 collective-permute-start.3
  155.9 5.4 collective-permute-done.2
  164.3 1.3 fusion.96
  165.8 1.3 multiply_reduce_fusion.1
  168.4 1.3 fusion.95
  170.0 1.3 multiply_reduce_fusion.2
  172.7 1.3 fusion.97
  174.3 1.3 fusion.94
  175.8 1.3 multiply_reduce_fusion
  180.0 1.3 multiply_reduce_fusion.3
  184.8 0.9 pad_add_fusion.4
  186.6 0.9 pad_add_fusion.6
  187.5 0.9 pad_add_fusion.7
  188.4 1.9 concatenate.44
  190.5 2.9 collective-permute-start.5
  193.9 2.9 collective-permute-done.4
  196.9 1.9 collective-permute-start.6
  198.8 11.5 collective-permute-start.7
  211.6 9.2 collective-permute-done.6
  221.8 2.0 add_select_fusion
  223.8 1.5 scatter-add.35
  226.5 1.4 fusion
  227.9 3.3 copy.103
  231.3 1.4 dynamic-slice.70
  233.5 15.4 all_gather.7
  248.9 1.3 fusion.13
  250.2 1559.1 %all-reduce.107.cloned.1.call-done = f32[1024,3,256]{2,1,0:T(4,128)} async-done(((f32[1024,3,256]{2,1,0:T(4,128)}), f32[1024,3,256]{2,1,0:T(4,128)}) %all-reduce.107.cloned.1.call-update) | async-done | bytes 3145744
  (142 shorter events, 22.4 us)
Async XLA Ops:
  7.2 128.4 %copy-start = (bf16[8,16,1024]{2,1,0:T(8,128)(2,1)S(1)}, bf16[8,16,1024]{2,1,0:T(8,128)(2,1)}, u32[]{:S(2)}) copy-start(bf16[8,16,1024]{2,1,0:T(8,128)(2,1)} %param.19) | copy-start | bytes 786436
  7.2 128.3 %all-gather.2.cloned.1.call-start = ((), (), s32[]{:S(2)}) async-start(), calls=%async_computation | async-start | bytes 7864320 | tf_op jit(solution)/shard_map/all_gather | solution.py:55
  7.9 1801.4 %all-reduce.107.cloned.1.call-start = ((), (), s32[]{:S(2)}) async-start(), calls=%async_computation.1 | async-start | bytes 8388608
  137.3 17.8 copy-start.15
  137.5 5.3 collective-permute-start
  138.0 5.2 collective-permute-start.1
  143.2 18.1 collective-permute-start.2
  146.6 14.7 collective-permute-start.3
  164.2 8.4 copy-start.13
  164.2 1.5 copy-start.6
  172.1 38.7 %copy-start.9 = (bf16[8,16,64]{2,1,0:T(8,128)(2,1)}, bf16[8,16,64]{2,1,0:T(8,128)(2,1)S(1)}, u32[]{:S(2)}) copy-start(bf16[8,16,64]{2,1,0:T(8,128)(2,1)S(1)} %convolution_bitcast_fusion.15) | copy-start | bytes 49156
  174.3 2.9 copy-start.4
  181.7 1.7 copy-start.2
  190.3 3.1 copy-start.14
  190.5 19.9 %copy-start.3 = (bf16[13,8,16,28]{3,2,0,1:T(8,128)(2,1)S(1)}, bf16[13,8,16,28]{3,2,0,1:T(8,128)(2,1)}, u32[]{:S(2)}) copy-start(bf16[13,8,16,28]{3,2,0,1:T(8,128)(2,1)} %copy-done.2) | copy-start | bytes 279556
  190.5 19.9 %copy-start.5 = (bf16[13,8,28,64]{3,2,0,1:T(8,128)(2,1)S(1)}, bf16[13,8,28,64]{3,2,0,1:T(8,128)(2,1)}, u32[]{:S(2)}) copy-start(bf16[13,8,28,64]{3,2,0,1:T(8,128)(2,1)} %copy-done.4) | copy-start | bytes 1118212
  190.5 6.3 collective-permute-start.4
  190.5 6.3 collective-permute-start.5
  193.9 16.9 copy-start.11
  196.9 23.9 %collective-permute-start.6 = (bf16[32,6,512]{2,1,0:T(8,128)(2,1)S(1)}, bf16[32,6,512]{2,1,0:T(8,128)(2,1)S(1)}, u32[]{:S(2)}, u32[]{:S(2)}) collective-permute-start(bf16[32,6,512]{2,1,0:T(8,128)(2,1)S(1)} %get-tuple-element.208), channel_id=1, source_target_pairs={{0,4},{4,8},{8,12},{12,16},{16,20},{20,24},{24,28},{28,32},{32,36}... | collective-permute-start | bytes 589832 | tf_op jit(solution)/shard_map/ppermute | solution.py:18
  198.8 22.0 %collective-permute-start.7 = (bf16[32,6,512]{2,1,0:T(8,128)(2,1)S(1)}, bf16[32,6,512]{2,1,0:T(8,128)(2,1)S(1)}, u32[]{:S(2)}, u32[]{:S(2)}) collective-permute-start(bf16[32,6,512]{2,1,0:T(8,128)(2,1)S(1)} %get-tuple-element.209), channel_id=1, source_target_pairs={{4,0},{8,4},{12,8},{16,12},{20,16},{24,20},{28,24},{32,28},{36,32}... | collective-permute-start | bytes 589832 | tf_op jit(solution)/shard_map/ppermute | solution.py:21
  225.9 0.6 copy-start.7
  231.2 2.1 copy-start.10
  231.2 2.1 copy-start.12
  231.2 2.2 copy-start.8
  231.2 17.7 copy-start.1
Sparse Core Ops, SparseCore 0:
  10.1 125.3 all-gather.1
  231.4 1577.8 all-reduce.106
where the time goes:
time: 1820 us
  waiting for transfers between devices  1710 us (94%)
  starting transfers between devices  31.2 us (2%)
  matrix products  20.7 us (1%)
    unnamed x3, waiting for transfers between devices  1560 us
    all_gather x1, waiting for transfers between devices, shards(): lax.all_gather(weight, 'fsdp', axis=1, tiled=True)  127 us
  transfers between devices with their start and end apart: 10, of which 7 were waited for; matrix products, arithmetic and copies ran while one was open for 0% of the time, Pallas kernels for 0%

commit v1 on v0

v1 whole, which is shorter than its diff:
```python
import functools
import math

import jax
import jax.numpy as jnp
from jax import lax
from jax.experimental import pallas as pl
from jax.experimental.pallas import tpu as pltpu
from jax.sharding import PartitionSpec as P

HEADS = 16
RADIUS = 6
MESH = pl.DeviceIdType.MESH
BF16 = jnp.bfloat16
F32 = jnp.float32

ROWS, COLS = 8, 16
TOK = ROWS * COLS
BLOCKS = 6
EXT = BLOCKS * TOK
SLAB = RADIUS * ROWS
EAST, WEST = 0, 64
LATS, LONS, FSDP = 8, 16, 4
XS, YS, ZS = 4, 8, 8

NORTH_SOUTH, EAST_WEST, CORNERS = 0, 2, 4
GRADS = 8
WEIGHTS, CORE_WEIGHTS = 16, 19
STATS = 22
CORE_GRAD = 30
INPUT_SUMS = 31
SUM_X, SUM_Y, SUM_Z = 34, 37, 44
COPIES = 45


def dot(a, b, ca, cb, precision=None):
    return lax.dot_general(
        a, b, (((ca,), (cb,)), ((), ())), preferred_element_type=F32, precision=precision
    )


def place(block, spot):
    half = spot // 64
    inner = spot % 64
    side_col = inner // ROWS + jnp.where(half == 0, COLS, -RADIUS)
    is_tile = block < 3
    row = jnp.where(is_tile, spot // COLS, inner % ROWS)
    col = jnp.where(is_tile, spot % COLS, side_col)
    kind = block % 3
    shift = jnp.where(kind == 1, -ROWS, jnp.where(kind == 2, ROWS, 0))
    real = is_tile | (inner < SLAB)
    return row + shift, col, real


def bias_of(block, spot, own, lat):
    row, col, real = place(block, spot)
    own_row, own_col = own // COLS, own % COLS
    gap_r = row - own_row
    gap_c = col - own_col
    grid_row = lat * ROWS + row
    allowed = (
        real
        & (gap_r <= RADIUS)
        & (gap_r >= -RADIUS)
        & (gap_c <= RADIUS)
        & (gap_c >= -RADIUS)
        & (grid_row >= 0)
        & (grid_row < LATS * ROWS)
    )
    return jnp.where(allowed, 0.0, -jnp.inf).astype(F32)


def kernel(
    tokens,
    grad_out,
    weight,
    grad_input,
    grad_weight,
    xs,
    dos,
    packs,
    wbuf,
    qkv,
    bias_f,
    bias_b,
    stats,
    stats_in,
    stat_rows,
    grads,
    x2,
    acc,
    gi_own,
    gi_out,
    gi_in,
    gx_out,
    gx_in,
    r1,
    gy_out,
    gy_in,
    r2,
    gz_in,
    send_sems,
    recv_sems,
    local_sems,
):
    lat = lax.axis_index("lat")
    lon = lax.axis_index("lon")
    fsdp = lax.axis_index("fsdp")
    x, core = lat // 2, lat % 2
    z_hi, y = lon // YS, lon % YS
    z = z_hi * FSDP + fsdp
    head_size = 64
    own_heads = HEADS // FSDP
    own_cols = own_heads * head_size
    width = FSDP * own_cols
    scale = 1.0 / math.sqrt(head_size)

    def at(*, d_lat=None, d_lon=None, d_fsdp=None):
        return (
            lat if d_lat is None else d_lat,
            lon if d_lon is None else d_lon,
            fsdp if d_fsdp is None else d_fsdp,
        )

    south_lat, north_lat = (lat + 1) % LATS, (lat + LATS - 1) % LATS
    east_lon, west_lon = (lon + 1) % LONS, (lon + LONS - 1) % LONS
    east_fsdp = jnp.where(y == YS - 1, FSDP - 1 - fsdp, fsdp)
    west_fsdp = jnp.where(y == 0, FSDP - 1 - fsdp, fsdp)
    south, north = at(d_lat=south_lat), at(d_lat=north_lat)
    east, west = at(d_lon=east_lon), at(d_lon=west_lon)
    east_copy = at(d_lon=east_lon, d_fsdp=east_fsdp)
    west_copy = at(d_lon=west_lon, d_fsdp=west_fsdp)
    other_core = at(d_lat=lat + 1 - 2 * core)

    def on_z(step):
        target = (z + step + ZS) % ZS
        return at(d_lon=(target // FSDP) * YS + y, d_fsdp=target % FSDP)

    def on_x(step):
        return at(d_lat=((x + step) % XS) * 2 + core)

    def on_y(step):
        return at(d_lon=z_hi * YS + (y + step) % YS)

    z_partner = at(d_lon=(1 - z_hi) * YS + y)
    corners = (
        at(d_lat=north_lat, d_lon=east_lon),
        at(d_lat=north_lat, d_lon=west_lon),
        at(d_lat=south_lat, d_lon=east_lon),
        at(d_lat=south_lat, d_lon=west_lon),
    )
    partners = [south, north, east, west, east_copy, west_copy, *corners]
    partners += [on_z(step) for step in (1, -1, 2, -2)]
    partners += [at(d_fsdp=(fsdp + step) % FSDP) for step in range(1, FSDP)]
    partners += [on_x(step) for step in range(1, XS)]
    partners += [on_y(step) for step in range(1, YS)]
    partners += [z_partner]

    barrier = pltpu.get_barrier_semaphore()
    for partner in partners:
        pl.semaphore_signal(barrier, inc=1, device_id=partner, device_id_type=MESH)

    own_tokens = pltpu.make_async_copy(tokens, xs.at[pl.ds(0, TOK)], local_sems.at[0])
    own_grads = pltpu.make_async_copy(grad_out, dos.at[pl.ds(0, TOK)], local_sems.at[1])
    own_start = pl.multiple_of(fsdp * own_cols, own_cols)
    own_weight = pltpu.make_async_copy(
        weight.at[:, :, pl.ds(own_start, own_cols)],
        wbuf.at[:, pl.ds(own_start, own_cols), :],
        local_sems.at[2],
    )
    own_tokens.start()
    own_grads.start()
    own_weight.start()

    def remote(src, dst, number, device):
        return pltpu.make_async_remote_copy(
            src_ref=src,
            dst_ref=dst,
            send_sem=send_sems.at[number],
            recv_sem=recv_sems.at[number],
            device_id=device,
            device_id_type=MESH,
        )

    pl.semaphore_wait(barrier, len(partners))

    sent = []

    def start(*args):
        copy = remote(*args)
        copy.start()
        sent.append(copy)
        return copy

    half_rows = own_cols // 2
    far = 2 - 4 * core
    weight_copies = []
    for number, step in enumerate((1, -1, far)):
        target = on_z(step)
        cols = pl.multiple_of(target[2] * own_cols, own_cols)
        rows = pl.multiple_of(fsdp * own_cols + core * half_rows, half_rows)
        weight_copies.append(
            start(
                weight.at[:, pl.ds(core * half_rows, half_rows), pl.ds(cols, own_cols)],
                wbuf.at[:, pl.ds(rows, half_rows), :],
                WEIGHTS + number,
                target,
            )
        )

    own_tokens.wait()
    own_grads.wait()
    tile_copies = []
    for number, device, block in ((0, south, 1), (1, north, 2)):
        tile_copies.append(
            start(
                xs.at[pl.ds(0, TOK)], xs.at[pl.ds(block * TOK, TOK)], NORTH_SOUTH + number, device
            )
        )
    spot = lax.broadcasted_iota(jnp.int32, (TOK, TOK), 0)
    flat = lax.broadcasted_iota(jnp.int32, (TOK, TOK), 1)
    inner = spot % 64
    source = (inner % ROWS) * COLS + inner // ROWS + jnp.where(spot < 64, 0, COLS - RADIUS)
    picks = (inner < SLAB) & (flat == source)
    pick = jnp.where(picks, 1.0, 0.0).astype(F32)
    pick_16 = pick.astype(BF16)
    packs[:, pl.ds(0, width)] = dot(pick_16, xs[pl.ds(0, TOK), :], 1, 0).astype(BF16)
    packs[:, pl.ds(width, own_cols)] = dot(pick_16, dos[pl.ds(0, TOK), :], 1, 0).astype(BF16)
    side_copies = []
    side = 3 * TOK
    for number, spot_at, token_device in ((0, EAST, west_copy), (1, WEST, east_copy)):
        side_copies.append(
            start(
                packs.at[pl.ds(spot_at, SLAB), pl.ds(0, width)],
                xs.at[pl.ds(side + spot_at, SLAB)],
                EAST_WEST + number,
                token_device,
            )
        )
    grad_tile_copies = []
    grad_side_copies = []
    for number, spot_at, device in ((0, EAST, west), (1, WEST, east)):
        grad_side_copies.append(
            start(
                packs.at[pl.ds(spot_at, SLAB), pl.ds(width, own_cols)],
                dos.at[pl.ds(side + spot_at, SLAB)],
                GRADS + EAST_WEST + number,
                device,
            )
        )
    for number, device, block in ((0, south, 1), (1, north, 2)):
        grad_tile_copies.append(
            start(
                dos.at[pl.ds(0, TOK)],
                dos.at[pl.ds(block * TOK, TOK)],
                GRADS + NORTH_SOUTH + number,
                device,
            )
        )

    for block in range(3, BLOCKS):
        for spot_at in (EAST, WEST):
            unused = pl.ds(block * TOK + spot_at + SLAB, 64 - SLAB)
            xs[unused, :] = jnp.zeros((64 - SLAB, width), BF16)
            dos[unused, :] = jnp.zeros((64 - SLAB, own_cols), BF16)

    @pl.loop(0, BLOCKS)
    def _(block):
        first = pl.multiple_of(block * TOK, TOK)
        bias_f[pl.ds(first, TOK), :] = bias_of(block, spot, flat, lat)
        bias_b[:, pl.ds(first, TOK)] = bias_of(block, flat, spot, lat)

    corner_copies = []
    for number, spot_at in ((0, EAST), (1, WEST)):
        side_copies[number].wait_recv()
        for leg, (device, block) in enumerate(((south, 4), (north, 5))):
            corner_copies.append(
                start(
                    xs.at[pl.ds(side + spot_at, SLAB)],
                    xs.at[pl.ds(block * TOK + spot_at, SLAB)],
                    CORNERS + 2 * number + leg,
                    device,
                )
            )
    core_weight_copies = []
    for number, step in enumerate((-1, 1, -far)):
        weight_copies[number].wait_recv()
        origin = (fsdp + step + FSDP) % FSDP
        rows = pl.multiple_of(origin * own_cols + core * half_rows, half_rows)
        region = wbuf.at[:, pl.ds(rows, half_rows), :]
        core_weight_copies.append(start(region, region, CORE_WEIGHTS + number, other_core))
    for number, spot_at in ((0, EAST), (1, WEST)):
        grad_side_copies[number].wait_recv()
        for leg, (device, block) in enumerate(((south, 4), (north, 5))):
            corner_copies.append(
                start(
                    dos.at[pl.ds(side + spot_at, SLAB)],
                    dos.at[pl.ds(block * TOK + spot_at, SLAB)],
                    GRADS + CORNERS + 2 * number + leg,
                    device,
                )
            )

    own_weight.wait()
    for copy in tile_copies + core_weight_copies + corner_copies[:4]:
        copy.wait_recv()

    @pl.loop(0, EXT // 256)
    def _(step):
        rows = pl.ds(pl.multiple_of(step * 256, 256), 256)
        block = xs[rows, :]
        for number in range(3):
            qkv[number, rows, :] = dot(block, wbuf[number], 1, 0).astype(BF16)

    lane = lax.broadcasted_iota(jnp.int32, (TOK, own_cols), 1) // head_size
    own = pl.ds(0, TOK)

    stats[pl.ds(3 * own_heads, own_heads), :] = jnp.zeros((own_heads, TOK), F32)

    @pl.loop(0, own_heads)
    def _(head):
        mine = lane == head
        query = jnp.where(mine, qkv[0, own, :], 0).astype(BF16)
        cotangent = jnp.where(mine, dos[own, :], 0).astype(BF16)
        scores = dot(qkv[1], query, 1, 1) * scale + bias_f[...]
        row_max = jnp.max(scores, axis=0, keepdims=True)
        prob = jnp.exp(scores - row_max)
        inv_sum = 1.0 / jnp.sum(prob, axis=0, keepdims=True)
        prob = prob * inv_sum
        grad_prob = dot(qkv[2], cotangent, 1, 1)
        delta = jnp.sum(prob * grad_prob, axis=0, keepdims=True)
        grad_score = (scale * (prob * (grad_prob - delta))).astype(BF16)
        part = dot(grad_score, qkv[1], 0, 0)
        acc[0] = jnp.where(mine, part, acc[0])
        stats[pl.ds(head, 1), :] = row_max
        stats[pl.ds(own_heads + head, 1), :] = inv_sum
        stats[pl.ds(2 * own_heads + head, 1), :] = delta

    stats[pl.ds(16, 16), :] = dot(
        stats[pl.ds(0, 16), :], pick, 1, 1, precision=lax.Precision.HIGHEST
    )
    tile_stats = stats.at[pl.ds(0, 16)]
    side_stats = stats.at[pl.ds(16, 16)]
    stat_copies = []
    for number, (src, device) in enumerate(
        (
            (tile_stats, south),
            (tile_stats, north),
            (side_stats, west),
            (side_stats, east),
            (side_stats, corners[3]),
            (side_stats, corners[2]),
            (side_stats, corners[1]),
            (side_stats, corners[0]),
        )
    ):
        stat_copies.append(start(src, stats_in.at[number], STATS + number, device))
    for copy in grad_tile_copies + corner_copies[4:] + stat_copies:
        copy.wait_recv()
    half_lane = lax.broadcasted_iota(jnp.int32, (16, TOK), 1) < 64
    stat_rows[:, pl.ds(0, TOK)] = stats[pl.ds(0, 16), :]
    stat_rows[:, pl.ds(TOK, TOK)] = stats_in[0]
    stat_rows[:, pl.ds(2 * TOK, TOK)] = stats_in[1]
    for block in range(3):
        first = 2 + 2 * block
        stat_rows[:, pl.ds((3 + block) * TOK, TOK)] = jnp.where(
            half_lane, stats_in[first], stats_in[first + 1]
        )

    @pl.loop(0, own_heads)
    def _(head):
        mine = lane == head
        key = jnp.where(mine, qkv[1, own, :], 0).astype(BF16)
        value = jnp.where(mine, qkv[2, own, :], 0).astype(BF16)
        row_max = stat_rows[pl.ds(head, 1), :]
        inv_sum = stat_rows[pl.ds(own_heads + head, 1), :]
        delta = stat_rows[pl.ds(2 * own_heads + head, 1), :]
        scores = dot(key, qkv[0], 1, 1) * scale + bias_b[...]
        prob = jnp.exp(jnp.minimum(scores - row_max, 0.0)) * inv_sum
        grad_prob = dot(value, dos[...], 1, 1)
        grad_score = (scale * (prob * (grad_prob - delta))).astype(BF16)
        acc[1] = jnp.where(mine, dot(grad_score, qkv[0], 1, 0), acc[1])
        acc[2] = jnp.where(mine, dot(prob.astype(BF16), dos[...], 1, 0), acc[2])

    for number in range(3):
        grads[own, pl.ds(number * own_cols, own_cols)] = acc[number].astype(BF16)

    core_grad = start(grads.at[own], grads.at[pl.ds(TOK, TOK)], CORE_GRAD, other_core)

    def input_terms(owner):
        rows = pl.ds(pl.multiple_of(owner * own_cols, own_cols), own_cols)
        total = None
        for number in range(3):
            term = dot(
                grads[own, pl.ds(number * own_cols, own_cols)], wbuf[number, rows, :], 1, 1
            )
            total = term if total is None else total + term
        return total

    input_copies = []
    for step in range(1, FSDP):
        peer = (fsdp + step) % FSDP
        gi_out[step - 1] = input_terms(peer).astype(BF16)
        input_copies.append(
            start(gi_out.at[step - 1], gi_in.at[step - 1], INPUT_SUMS + step - 1, at(d_fsdp=peer))
        )
    gi_own[...] = input_terms(fsdp)

    x2[own, :] = xs[own, :]
    pair_rows = pl.ds(pl.multiple_of((2 - core) * TOK, TOK), TOK)
    x2[pl.ds(TOK, TOK), :] = xs[pair_rows, :]
    core_grad.wait_recv()

    def weight_terms(owner):
        cols = pl.ds(pl.multiple_of(owner * TOK, TOK), TOK)
        return dot(x2[:, cols], grads[...], 0, 0)

    x_copies = []
    for step in range(1, XS):
        owner = ((x + step) % XS) * 2 + core
        gx_out[step - 1] = weight_terms(owner).astype(BF16)
        x_copies.append(
            start(gx_out.at[step - 1], gx_in.at[step - 1], SUM_X + step - 1, on_x(step))
        )
    total = weight_terms(lat)
    for copy in input_copies:
        copy.wait_recv()
    grad_input[...] = (
        gi_own[...] + gi_in[0].astype(F32) + gi_in[1].astype(F32) + gi_in[2].astype(F32)
    ).astype(BF16)
    for copy in x_copies:
        copy.wait_recv()
    r1[...] = total + (
        gx_in[0].astype(F32) + gx_in[1].astype(F32) + gx_in[2].astype(F32)
    )

    def both_halves(owner):
        low = r1[pl.ds(pl.multiple_of(owner * 8, 8), 8), :]
        high = r1[pl.ds(pl.multiple_of(YS * 8 + owner * 8, 8), 8), :]
        return jnp.concatenate([low, high], axis=0)

    y_copies = []
    for step in range(1, YS):
        gy_out[step - 1] = both_halves((y + step) % YS).astype(BF16)
        y_copies.append(
            start(gy_out.at[step - 1], gy_in.at[step - 1], SUM_Y + step - 1, on_y(step))
        )
    total = both_halves(y)
    for number, copy in enumerate(y_copies):
        copy.wait_recv()
        total = total + gy_in[number].astype(F32)
    r2[...] = total
    z_copy = start(
        r2.at[pl.ds(pl.multiple_of((1 - z_hi) * 8, 8), 8)], gz_in, SUM_Z, z_partner
    )
    z_copy.wait_recv()
    result = r2[pl.ds(pl.multiple_of(z_hi * 8, 8), 8), :] + gz_in[...]
    weight_scale = 1.0 / math.sqrt(TOK * LATS * LONS)
    for number in range(3):
        grad_weight[number] = result[:, number * own_cols : (number + 1) * own_cols] * weight_scale

    for copy in sent:
        copy.wait_send()


def shards(tokens, grad_out, weight):
    rows, cols, width = tokens.shape
    own_cols = grad_out.shape[2]
    three = weight.shape[0]
    anywhere = pl.BlockSpec(memory_space=pl.ANY)
    in_vmem = pl.BlockSpec(memory_space=pltpu.VMEM)
    total = three * own_cols
    grad_input, grad_weight = pl.pallas_call(
        kernel,
        out_shape=(
            jax.ShapeDtypeStruct((TOK, own_cols), BF16),
            jax.ShapeDtypeStruct((three, 8, own_cols), F32),
        ),
        in_specs=[anywhere] * 3,
        out_specs=(in_vmem, in_vmem),
        scratch_shapes=[
            pltpu.VMEM((EXT, width), BF16),
            pltpu.VMEM((EXT, own_cols), BF16),
            pltpu.VMEM((TOK, width + own_cols), BF16),
            pltpu.VMEM((three, width, own_cols), BF16),
            pltpu.VMEM((three, EXT, own_cols), BF16),
            pltpu.VMEM((EXT, TOK), F32),
            pltpu.VMEM((TOK, EXT), F32),
            pltpu.VMEM((32, TOK), F32),
            pltpu.VMEM((8, 16, TOK), F32),
            pltpu.VMEM((16, EXT), F32),
            pltpu.VMEM((2 * TOK, total), BF16),
            pltpu.VMEM((2 * TOK, width), BF16),
            pltpu.VMEM((three, TOK, own_cols), F32),
            pltpu.VMEM((TOK, own_cols), F32),
            pltpu.VMEM((FSDP - 1, TOK, own_cols), BF16),
            pltpu.VMEM((FSDP - 1, TOK, own_cols), BF16),
            pltpu.VMEM((XS - 1, TOK, total), BF16),
            pltpu.VMEM((XS - 1, TOK, total), BF16),
            pltpu.VMEM((TOK, total), F32),
            pltpu.VMEM((YS - 1, 16, total), BF16),
            pltpu.VMEM((YS - 1, 16, total), BF16),
            pltpu.VMEM((16, total), F32),
            pltpu.VMEM((8, total), F32),
            pltpu.SemaphoreType.DMA((COPIES,)),
            pltpu.SemaphoreType.DMA((COPIES,)),
            pltpu.SemaphoreType.DMA((3,)),
        ],
        compiler_params=pltpu.CompilerParams(
            collective_id=0, has_side_effects=True, vmem_limit_bytes=48 * 1024 * 1024
        ),
    )(tokens.reshape(TOK, width), grad_out.reshape(TOK, own_cols), weight)
    return grad_input.reshape(rows, cols, own_cols), grad_weight


def solution(mesh):
    placed = (P("lat", "lon", None), P("lat", "lon", "fsdp"), P(None, "fsdp", None))
    return jax.shard_map(
        shards,
        mesh=mesh,
        in_specs=placed,
        out_specs=(P("lat", "lon", "fsdp"), P(None, ("lat", "lon"), "fsdp")),
        check_vma=False,
    )
```

time: 1820 us -> 72.5 us (0.04)
  the two profiles are of different devices: /device:TPU:64 before, /device:TPU:88 now
where the time goes in v1:
time: 72.5 us; the launch traced here: 72.3 us
  Pallas kernels  67.2 us (93%)
  local copies, waits for them, and re-layouts  4.43 us (6%)
    pallas_call x1, Pallas kernels, shards(): pl.pallas_call(kernel, out_shape=(jax.ShapeDtypeStruct((TOK, own_cols), B...  67.2 us
    unnamed x8, local copies, waits for them, and re-layouts  4.43 us

profile of v1, /device:TPU:88, one launch (start us, length us, event | category | flops | bytes accessed | tf_op | source)
XLA Modules:
  0.0 72.3 jit_solution(5435263026309959471)
XLA Ops:
  0.6 0.0 copy-start
  0.6 1.4 %copy-done = bf16[3,256,1024]{2,1,0:T(8,128)(2,1)S(1)} copy-done((bf16[3,256,1024]{2,1,0:T(8,128)(2,1)S(1)}, bf16[3,256,1024]{2,1,0:T(8,128)(2,1)}, u32[]{:S(2)}) %copy-start) | copy-done | bytes 1572888
  2.0 0.0 copy-start.1
  2.0 0.9 %copy-done.1 = bf16[8,16,1024]{2,1,0:T(8,128)(2,1)S(1)} copy-done((bf16[8,16,1024]{2,1,0:T(8,128)(2,1)S(1)}, bf16[8,16,1024]{2,1,0:T(8,128)(2,1)}, u32[]{:S(2)}) %copy-start.1) | copy-done | bytes 262168
  3.0 0.0 copy-start.2
  3.0 0.8 %copy-done.2 = bf16[8,16,256]{2,1,0:T(8,128)(2,1)S(1)} copy-done((bf16[8,16,256]{2,1,0:T(8,128)(2,1)S(1)}, bf16[8,16,256]{2,1,0:T(8,128)(2,1)}, u32[]{:S(2)}) %copy-start.2) | copy-done | bytes 65560
  3.8 67.2 %shard_map.50 = (bf16[128,256]{1,0:T(8,128)(2,1)S(1)}, f32[3,8,256]{2,1,0:T(8,128)S(1)}) custom-call(bf16[128,1024]{1,0:T(8,128)(2,1)S(1)} %bitcast.3, bf16[128,256]{1,0:T(8,128)(2,1)S(1)} %bitcast.5, bf16[3,256,1024]{2,1,0:T(8,128)(2,1)S(1)} %copy-done), custom_call_target="tpu_custom_call" | custom-call | tf_op jit(solution)/shard_map/pallas_call | solution.py:473
  71.1 0.6 copy.7
  71.7 0.6 copy.8
Async XLA Ops:
  0.6 1.4 %copy-start = (bf16[3,256,1024]{2,1,0:T(8,128)(2,1)S(1)}, bf16[3,256,1024]{2,1,0:T(8,128)(2,1)}, u32[]{:S(2)}) copy-start(bf16[3,256,1024]{2,1,0:T(8,128)(2,1)} %weight.1) | copy-start | bytes 4718596
  2.0 0.9 %copy-start.1 = (bf16[8,16,1024]{2,1,0:T(8,128)(2,1)S(1)}, bf16[8,16,1024]{2,1,0:T(8,128)(2,1)}, u32[]{:S(2)}) copy-start(bf16[8,16,1024]{2,1,0:T(8,128)(2,1)} %param.3) | copy-start | bytes 786436
  3.0 0.8 %copy-start.2 = (bf16[8,16,256]{2,1,0:T(8,128)(2,1)S(1)}, bf16[8,16,256]{2,1,0:T(8,128)(2,1)}, u32[]{:S(2)}) copy-start(bf16[8,16,256]{2,1,0:T(8,128)(2,1)} %param.4) | copy-start | bytes 196612

commit v2 on v1

--- a/solution.py
+++ b/solution.py
@@ -28,9 +28,9 @@
 WEIGHTS, CORE_WEIGHTS = 16, 19
 STATS = 22
 CORE_GRAD = 30
-INPUT_SUMS = 31
-SUM_X, SUM_Y, SUM_Z = 34, 37, 44
-COPIES = 45
+INPUT_SUMS = 32
+SUM_X, SUM_Y, SUM_Z = 35, 41, 55
+COPIES = 57
 
 
 def dot(a, b, ca, cb, precision=None):
@@ -98,6 +98,7 @@
     gy_out,
     gy_in,
     r2,
+    gz_out,
     gz_in,
     send_sems,
     recv_sems,
@@ -182,6 +183,17 @@
             device_id_type=MESH,
         )
 
+    own_tokens.wait()
+    own_grads.wait()
+    spot = lax.broadcasted_iota(jnp.int32, (TOK, TOK), 0)
+    flat = lax.broadcasted_iota(jnp.int32, (TOK, TOK), 1)
+    inner = spot % 64
+    source = (inner % ROWS) * COLS + inner // ROWS + jnp.where(spot < 64, 0, COLS - RADIUS)
+    picks = (inner < SLAB) & (flat == source)
+    pick = jnp.where(picks, 1.0, 0.0).astype(F32)
+    pick_16 = pick.astype(BF16)
+    packs[:, pl.ds(0, width)] = dot(pick_16, xs[pl.ds(0, TOK), :], 1, 0).astype(BF16)
+    packs[:, pl.ds(width, own_cols)] = dot(pick_16, dos[pl.ds(0, TOK), :], 1, 0).astype(BF16)
     pl.semaphore_wait(barrier, len(partners))
 
     sent = []
@@ -192,6 +204,17 @@
         sent.append(copy)
         return copy
 
+    side_copies = []
+    side = 3 * TOK
+    for number, spot_at, token_device in ((0, EAST, west_copy), (1, WEST, east_copy)):
+        side_copies.append(
+            start(
+                packs.at[pl.ds(spot_at, SLAB), pl.ds(0, width)],
+                xs.at[pl.ds(side + spot_at, SLAB)],
+                EAST_WEST + number,
+                token_device,
+            )
+        )
     half_rows = own_cols // 2
     far = 2 - 4 * core
     weight_copies = []
@@ -208,8 +231,6 @@
             )
         )
 
-    own_tokens.wait()
-    own_grads.wait()
     tile_copies = []
     for number, device, block in ((0, south, 1), (1, north, 2)):
         tile_copies.append(
@@ -217,37 +238,7 @@
                 xs.at[pl.ds(0, TOK)], xs.at[pl.ds(block * TOK, TOK)], NORTH_SOUTH + number, device
             )
         )
-    spot = lax.broadcasted_iota(jnp.int32, (TOK, TOK), 0)
-    flat = lax.broadcasted_iota(jnp.int32, (TOK, TOK), 1)
-    inner = spot % 64
-    source = (inner % ROWS) * COLS + inner // ROWS + jnp.where(spot < 64, 0, COLS - RADIUS)
-    picks = (inner < SLAB) & (flat == source)
-    pick = jnp.where(picks, 1.0, 0.0).astype(F32)
-    pick_16 = pick.astype(BF16)
-    packs[:, pl.ds(0, width)] = dot(pick_16, xs[pl.ds(0, TOK), :], 1, 0).astype(BF16)
-    packs[:, pl.ds(width, own_cols)] = dot(pick_16, dos[pl.ds(0, TOK), :], 1, 0).astype(BF16)
-    side_copies = []
-    side = 3 * TOK
-    for number, spot_at, token_device in ((0, EAST, west_copy), (1, WEST, east_copy)):
-        side_copies.append(
-            start(
-                packs.at[pl.ds(spot_at, SLAB), pl.ds(0, width)],
-                xs.at[pl.ds(side + spot_at, SLAB)],
-                EAST_WEST + number,
-                token_device,
-            )
-        )
     grad_tile_copies = []
-    grad_side_copies = []
-    for number, spot_at, device in ((0, EAST, west), (1, WEST, east)):
-        grad_side_copies.append(
-            start(
-                packs.at[pl.ds(spot_at, SLAB), pl.ds(width, own_cols)],
-                dos.at[pl.ds(side + spot_at, SLAB)],
-                GRADS + EAST_WEST + number,
-                device,
-            )
-        )
     for number, device, block in ((0, south, 1), (1, north, 2)):
         grad_tile_copies.append(
             start(
@@ -289,20 +280,19 @@
         rows = pl.multiple_of(origin * own_cols + core * half_rows, half_rows)
         region = wbuf.at[:, pl.ds(rows, half_rows), :]
         core_weight_copies.append(start(region, region, CORE_WEIGHTS + number, other_core))
-    for number, spot_at in ((0, EAST), (1, WEST)):
-        grad_side_copies[number].wait_recv()
-        for leg, (device, block) in enumerate(((south, 4), (north, 5))):
-            corner_copies.append(
-                start(
-                    dos.at[pl.ds(side + spot_at, SLAB)],
-                    dos.at[pl.ds(block * TOK + spot_at, SLAB)],
-                    GRADS + CORNERS + 2 * number + leg,
-                    device,
-                )
-            )
+    grad_side_copies = []
+    for number, spot_at, device in ((0, EAST, west), (1, WEST, east)):
+        grad_side_copies.append(
+            start(
+                packs.at[pl.ds(spot_at, SLAB), pl.ds(width, own_cols)],
+                dos.at[pl.ds(side + spot_at, SLAB)],
+                GRADS + EAST_WEST + number,
+                device,
+            )
+        )
 
     own_weight.wait()
-    for copy in tile_copies + core_weight_copies + corner_copies[:4]:
+    for copy in tile_copies + core_weight_copies + corner_copies:
         copy.wait_recv()
 
     @pl.loop(0, EXT // 256)
@@ -355,7 +345,129 @@
         )
     ):
         stat_copies.append(start(src, stats_in.at[number], STATS + number, device))
-    for copy in grad_tile_copies + corner_copies[4:] + stat_copies:
+
+    parts = ((0, own_cols), (own_cols, 2 * own_cols))
+    core_copies = []
+    x_copies = [[], []]
+    y_copies = [[], []]
+    z_copies = []
+
+    def share_with_core(part):
+        cols = pl.ds(*parts[part])
+        return start(
+            grads.at[own, cols],
+            grads.at[pl.ds(TOK, TOK), cols],
+            CORE_GRAD + part,
+            other_core,
+        )
+
+    def input_terms(owner, numbers):
+        rows = pl.ds(pl.multiple_of(owner * own_cols, own_cols), own_cols)
+        total = None
+        for number in numbers:
+            term = dot(
+                grads[own, pl.ds(number * own_cols, own_cols)], wbuf[number, rows, :], 1, 1
+            )
+            total = term if total is None else total + term
+        return total
+
+    def send_x(part):
+        core_copies[part].wait_recv()
+        cols = pl.ds(*parts[part])
+
+        def terms(owner):
+            rows = pl.ds(pl.multiple_of(owner * TOK, TOK), TOK)
+            return dot(x2[:, rows], grads[:, cols], 0, 0)
+
+        for step in range(1, XS):
+            gx_out[step - 1, :, cols] = terms(((x + step) % XS) * 2 + core).astype(BF16)
+            x_copies[part].append(
+                start(
+                    gx_out.at[step - 1, :, cols],
+                    gx_in.at[step - 1, :, cols],
+                    SUM_X + (XS - 1) * part + step - 1,
+                    on_x(step),
+                )
+            )
+        r1[:, cols] = terms(lat)
+
+    def send_y(part):
+        cols = pl.ds(*parts[part])
+        for copy in x_copies[part]:
+            copy.wait_recv()
+        total = r1[:, cols]
+        for number in range(XS - 1):
+            total = total + gx_in[number, :, cols].astype(F32)
+        r1[:, cols] = total
+        for step in range(1, YS):
+            gy_out[step - 1, :, cols] = both_halves((y + step) % YS, cols).astype(BF16)
+            y_copies[part].append(
+                start(
+                    gy_out.at[step - 1, :, cols],
+                    gy_in.at[step - 1, :, cols],
+                    SUM_Y + (YS - 1) * part + step - 1,
+                    on_y(step),
+                )
+            )
+
+    def both_halves(owner, cols):
+        low = r1[pl.ds(pl.multiple_of(owner * 8, 8), 8), cols]
+        high = r1[pl.ds(pl.multiple_of(YS * 8 + owner * 8, 8), 8), cols]
+        return jnp.concatenate([low, high], axis=0)
+
+    def send_z(part):
+        first, count = parts[part]
+        cols = pl.ds(first, count)
+        half = count // 2
+        total = both_halves(y, cols)
+        for number, copy in enumerate(y_copies[part]):
+            copy.wait_recv()
+            total = total + gy_in[number, :, cols].astype(F32)
+        r2[:, cols] = total
+        rows = pl.ds(pl.multiple_of((1 - z_hi) * 8, 8), 8)
+        folded = pl.ds(first // 2, half)
+        gz_out[:, folded] = jnp.concatenate(
+            [r2[rows, pl.ds(first, half)], r2[rows, pl.ds(first + half, half)]], axis=0
+        ).astype(BF16)
+        z_copies.append(
+            start(gz_out.at[:, folded], gz_in.at[:, folded], SUM_Z + part, z_partner)
+        )
+
+    def finish(part):
+        first, count = parts[part]
+        half = count // 2
+        z_copies[part].wait_recv()
+        other = gz_in[:, pl.ds(first // 2, half)].astype(F32)
+        own_rows = pl.ds(pl.multiple_of(z_hi * 8, 8), 8)
+        total = r2[own_rows, pl.ds(first, count)]
+        total = (total + jnp.concatenate([other[:8], other[8:]], axis=1)) * weight_scale
+        for number in range(count // own_cols):
+            grad_weight[first // own_cols + number] = total[
+                :, number * own_cols : (number + 1) * own_cols
+            ]
+
+    weight_scale = 1.0 / math.sqrt(TOK * LATS * LONS)
+    grads[own, pl.ds(0, own_cols)] = acc[0].astype(BF16)
+    core_copies.append(share_with_core(0))
+    x2[own, :] = xs[own, :]
+    pair_rows = pl.ds(pl.multiple_of((2 - core) * TOK, TOK), TOK)
+    x2[pl.ds(TOK, TOK), :] = xs[pair_rows, :]
+    for step in range(FSDP):
+        gi_own[step] = input_terms((fsdp + step) % FSDP, (0,))
+    send_x(0)
+    grad_corner_copies = []
+    for number, spot_at in ((0, EAST), (1, WEST)):
+        grad_side_copies[number].wait_recv()
+        for leg, (device, block) in enumerate(((south, 4), (north, 5))):
+            grad_corner_copies.append(
+                start(
+                    dos.at[pl.ds(side + spot_at, SLAB)],
+                    dos.at[pl.ds(block * TOK + spot_at, SLAB)],
+                    GRADS + CORNERS + 2 * number + leg,
+                    device,
+                )
+            )
+    for copy in grad_tile_copies + grad_corner_copies + stat_copies:
         copy.wait_recv()
     half_lane = lax.broadcasted_iota(jnp.int32, (16, TOK), 1) < 64
     stat_rows[:, pl.ds(0, TOK)] = stats[pl.ds(0, 16), :]
@@ -382,82 +494,30 @@
         acc[1] = jnp.where(mine, dot(grad_score, qkv[0], 1, 0), acc[1])
         acc[2] = jnp.where(mine, dot(prob.astype(BF16), dos[...], 1, 0), acc[2])
 
-    for number in range(3):
+    for number in (1, 2):
         grads[own, pl.ds(number * own_cols, own_cols)] = acc[number].astype(BF16)
-
-    core_grad = start(grads.at[own], grads.at[pl.ds(TOK, TOK)], CORE_GRAD, other_core)
-
-    def input_terms(owner):
-        rows = pl.ds(pl.multiple_of(owner * own_cols, own_cols), own_cols)
-        total = None
-        for number in range(3):
-            term = dot(
-                grads[own, pl.ds(number * own_cols, own_cols)], wbuf[number, rows, :], 1, 1
-            )
-            total = term if total is None else total + term
-        return total
+    core_copies.append(share_with_core(1))
 
     input_copies = []
     for step in range(1, FSDP):
         peer = (fsdp + step) % FSDP
-        gi_out[step - 1] = input_terms(peer).astype(BF16)
+        gi_out[step - 1] = (gi_own[step] + input_terms(peer, (1, 2))).astype(BF16)
         input_copies.append(
             start(gi_out.at[step - 1], gi_in.at[step - 1], INPUT_SUMS + step - 1, at(d_fsdp=peer))
         )
-    gi_own[...] = input_terms(fsdp)
-
-    x2[own, :] = xs[own, :]
-    pair_rows = pl.ds(pl.multiple_of((2 - core) * TOK, TOK), TOK)
-    x2[pl.ds(TOK, TOK), :] = xs[pair_rows, :]
-    core_grad.wait_recv()
-
-    def weight_terms(owner):
-        cols = pl.ds(pl.multiple_of(owner * TOK, TOK), TOK)
-        return dot(x2[:, cols], grads[...], 0, 0)
-
-    x_copies = []
-    for step in range(1, XS):
-        owner = ((x + step) % XS) * 2 + core
-        gx_out[step - 1] = weight_terms(owner).astype(BF16)
-        x_copies.append(
-            start(gx_out.at[step - 1], gx_in.at[step - 1], SUM_X + step - 1, on_x(step))
-        )
-    total = weight_terms(lat)
+    gi_own[0] = gi_own[0] + input_terms(fsdp, (1, 2))
+    send_x(1)
+    send_y(0)
     for copy in input_copies:
         copy.wait_recv()
     grad_input[...] = (
-        gi_own[...] + gi_in[0].astype(F32) + gi_in[1].astype(F32) + gi_in[2].astype(F32)
+        gi_own[0] + gi_in[0].astype(F32) + gi_in[1].astype(F32) + gi_in[2].astype(F32)
     ).astype(BF16)
-    for copy in x_copies:
-        copy.wait_recv()
-    r1[...] = total + (
-        gx_in[0].astype(F32) + gx_in[1].astype(F32) + gx_in[2].astype(F32)
-    )
-
-    def both_halves(owner):
-        low = r1[pl.ds(pl.multiple_of(owner * 8, 8), 8), :]
-        high = r1[pl.ds(pl.multiple_of(YS * 8 + owner * 8, 8), 8), :]
-        return jnp.concatenate([low, high], axis=0)
-
-    y_copies = []
-    for step in range(1, YS):
-        gy_out[step - 1] = both_halves((y + step) % YS).astype(BF16)
-        y_copies.append(
-            start(gy_out.at[step - 1], gy_in.at[step - 1], SUM_Y + step - 1, on_y(step))
-        )
-    total = both_halves(y)
-    for number, copy in enumerate(y_copies):
-        copy.wait_recv()
-        total = total + gy_in[number].astype(F32)
-    r2[...] = total
-    z_copy = start(
-        r2.at[pl.ds(pl.multiple_of((1 - z_hi) * 8, 8), 8)], gz_in, SUM_Z, z_partner
-    )
-    z_copy.wait_recv()
-    result = r2[pl.ds(pl.multiple_of(z_hi * 8, 8), 8), :] + gz_in[...]
-    weight_scale = 1.0 / math.sqrt(TOK * LATS * LONS)
-    for number in range(3):
-        grad_weight[number] = result[:, number * own_cols : (number + 1) * own_cols] * weight_scale
+    send_z(0)
+    send_y(1)
+    send_z(1)
+    finish(0)
+    finish(1)
 
     for copy in sent:
         copy.wait_send()
@@ -492,7 +552,7 @@
             pltpu.VMEM((2 * TOK, total), BF16),
             pltpu.VMEM((2 * TOK, width), BF16),
             pltpu.VMEM((three, TOK, own_cols), F32),
-            pltpu.VMEM((TOK, own_cols), F32),
+            pltpu.VMEM((FSDP, TOK, own_cols), F32),
             pltpu.VMEM((FSDP - 1, TOK, own_cols), BF16),
             pltpu.VMEM((FSDP - 1, TOK, own_cols), BF16),
             pltpu.VMEM((XS - 1, TOK, total), BF16),
@@ -501,13 +561,14 @@
             pltpu.VMEM((YS - 1, 16, total), BF16),
             pltpu.VMEM((YS - 1, 16, total), BF16),
             pltpu.VMEM((16, total), F32),
-            pltpu.VMEM((8, total), F32),
+            pltpu.VMEM((16, total // 2), BF16),
+            pltpu.VMEM((16, total // 2), BF16),
             pltpu.SemaphoreType.DMA((COPIES,)),
             pltpu.SemaphoreType.DMA((COPIES,)),
             pltpu.SemaphoreType.DMA((3,)),
         ],
         compiler_params=pltpu.CompilerParams(
-            collective_id=0, has_side_effects=True, vmem_limit_bytes=48 * 1024 * 1024
+            collective_id=0, has_side_effects=True, vmem_limit_bytes=63 * 1024 * 1024
         ),
     )(tokens.reshape(TOK, width), grad_out.reshape(TOK, own_cols), weight)
     return grad_input.reshape(rows, cols, own_cols), grad_weight

time: 72.5 us -> 68.1 us (0.939)
  the two profiles are of different devices: /device:TPU:88 before, /device:TPU:96 now
where the time goes in v2:
time: 68.1 us; the launch traced here: 67.9 us
  Pallas kernels  64.4 us (95%)
  local copies, waits for them, and re-layouts  2.82 us (4%)
    pallas_call x1, Pallas kernels, shards(): pl.pallas_call(kernel, out_shape=(jax.ShapeDtypeStruct((TOK, own_cols), B...  64.4 us
    unnamed x2, local copies, waits for them, and re-layouts  2.82 us

profile of v2, /device:TPU:96, one launch (start us, length us, event | category | flops | bytes accessed | tf_op | source)
XLA Modules:
  0.0 67.9 jit_solution(4773681033481978416)
XLA Ops:
  0.6 64.4 %shard_map.50 = (bf16[128,256]{1,0:T(8,128)(2,1)}, f32[3,8,256]{2,1,0:T(8,128)}) custom-call(bf16[128,1024]{1,0:T(8,128)(2,1)} %bitcast.3, bf16[128,256]{1,0:T(8,128)(2,1)} %bitcast.5, bf16[3,256,1024]{2,1,0:T(8,128)(2,1)} %weight.1), custom_call_target="tpu_custom_call" | custom-call | tf_op jit(solution)/shard_map/pallas_call | solution.py:533
  65.1 1.5 %copy.7 = bf16[8,16,256]{2,1,0:T(8,128)(2,1)} copy(bf16[8,16,256]{2,1,0:T(8,128)(2,1)} %bitcast.4) | data formatting | bytes 131072
  66.6 1.3 %copy.8 = f32[3,8,256]{2,1,0:T(8,128)} copy(f32[3,8,256]{2,1,0:T(8,128)} %get-tuple-element.9) | data formatting | bytes 49152

commit v3 on v2

--- a/solution.py
+++ b/solution.py
@@ -25,12 +25,12 @@
 
 NORTH_SOUTH, EAST_WEST, CORNERS = 0, 2, 4
 GRADS = 8
-WEIGHTS, CORE_WEIGHTS = 16, 19
-STATS = 22
-CORE_GRAD = 30
-INPUT_SUMS = 32
-SUM_X, SUM_Y, SUM_Z = 35, 41, 55
-COPIES = 57
+WEIGHTS, SIDE_WEIGHTS, CORE_WEIGHTS = 16, 19, 25
+STATS = 31
+CORE_GRAD = 39
+INPUT_SUMS = 42
+SUM_X, SUM_Y, SUM_Z = 45, 54, 75
+COPIES = 78
 
 
 def dot(a, b, ca, cb, precision=None):
@@ -87,7 +87,8 @@
     stats_in,
     stat_rows,
     grads,
-    x2,
+    xt,
+    probs,
     acc,
     gi_own,
     gi_out,
@@ -183,6 +184,61 @@
             device_id_type=MESH,
         )
 
+    pl.semaphore_wait(barrier, len(partners))
+
+    sent = []
+
+    def start(*args):
+        copy = remote(*args)
+        copy.start()
+        sent.append(copy)
+        return copy
+
+    half_rows = own_cols // 2
+    quarter = half_rows // 2
+    eighth = quarter // 2
+    parity = y % 2
+    far = 2 - 4 * core
+    mine_at = core * half_rows + parity * quarter
+    other_at = core * half_rows + (1 - parity) * quarter
+
+    def weight_rows(origin, offset, count):
+        first = pl.multiple_of(origin * own_cols + offset, eighth)
+        return wbuf.at[:, pl.ds(first, count), :]
+
+    weight_copies = []
+    for number, step in enumerate((1, -1, far)):
+        target = on_z(step)
+        cols = pl.multiple_of(target[2] * own_cols, own_cols)
+        weight_copies.append(
+            start(
+                weight.at[
+                    :, pl.ds(pl.multiple_of(mine_at, quarter), quarter), pl.ds(cols, own_cols)
+                ],
+                weight_rows(fsdp, mine_at, quarter),
+                WEIGHTS + number,
+                target,
+            )
+        )
+
+    tile_copies = []
+    for number, device, block in ((0, south, 1), (1, north, 2)):
+        tile_copies.append(
+            start(
+                tokens, xs.at[pl.ds(block * TOK, TOK)], NORTH_SOUTH + number, device
+            )
+        )
+    grad_tile_copies = []
+    for number, device, block in ((0, south, 1), (1, north, 2)):
+        grad_tile_copies.append(
+            start(
+                grad_out,
+                dos.at[pl.ds(block * TOK, TOK)],
+                GRADS + NORTH_SOUTH + number,
+                device,
+            )
+        )
+
     own_tokens.wait()
     own_grads.wait()
     spot = lax.broadcasted_iota(jnp.int32, (TOK, TOK), 0)
@@ -194,16 +250,6 @@
     pick_16 = pick.astype(BF16)
     packs[:, pl.ds(0, width)] = dot(pick_16, xs[pl.ds(0, TOK), :], 1, 0).astype(BF16)
     packs[:, pl.ds(width, own_cols)] = dot(pick_16, dos[pl.ds(0, TOK), :], 1, 0).astype(BF16)
-    pl.semaphore_wait(barrier, len(partners))
-
-    sent = []
-
-    def start(*args):
-        copy = remote(*args)
-        copy.start()
-        sent.append(copy)
-        return copy
-
     side_copies = []
     side = 3 * TOK
     for number, spot_at, token_device in ((0, EAST, west_copy), (1, WEST, east_copy)):
@@ -215,39 +261,7 @@
                 token_device,
             )
         )
-    half_rows = own_cols // 2
-    far = 2 - 4 * core
-    weight_copies = []
-    for number, step in enumerate((1, -1, far)):
-        target = on_z(step)
-        cols = pl.multiple_of(target[2] * own_cols, own_cols)
-        rows = pl.multiple_of(fsdp * own_cols + core * half_rows, half_rows)
-        weight_copies.append(
-            start(
-                weight.at[:, pl.ds(core * half_rows, half_rows), pl.ds(cols, own_cols)],
-                wbuf.at[:, pl.ds(rows, half_rows), :],
-                WEIGHTS + number,
-                target,
-            )
-        )
-
-    tile_copies = []
-    for number, device, block in ((0, south, 1), (1, north, 2)):
-        tile_copies.append(
-            start(
-                xs.at[pl.ds(0, TOK)], xs.at[pl.ds(block * TOK, TOK)], NORTH_SOUTH + number, device
-            )
-        )
-    grad_tile_copies = []
-    for number, device, block in ((0, south, 1), (1, north, 2)):
-        grad_tile_copies.append(
-            start(
-                dos.at[pl.ds(0, TOK)],
-                dos.at[pl.ds(block * TOK, TOK)],
-                GRADS + NORTH_SOUTH + number,
-                device,
-            )
-        )
+    xt[:, pl.ds(0, TOK)] = xs[pl.ds(0, TOK), :].T
 
     for block in range(3, BLOCKS):
         for spot_at in (EAST, WEST):
@@ -261,6 +275,18 @@
         bias_f[pl.ds(first, TOK), :] = bias_of(block, spot, flat, lat)
         bias_b[:, pl.ds(first, TOK)] = bias_of(block, flat, spot, lat)
 
+    side_weight_copies = []
+    core_weight_copies = []
+    origins = [(fsdp + step + FSDP) % FSDP for step in (-1, 1, -far)]
+    for number, origin in enumerate(origins):
+        weight_copies[number].wait_recv()
+        for leg, step in enumerate((1, -1)):
+            region = weight_rows(origin, mine_at + leg * eighth, eighth)
+            side_weight_copies.append(
+                start(region, region, SIDE_WEIGHTS + 2 * number + leg, on_y(step))
+            )
+        region = weight_rows(origin, mine_at, quarter)
+        core_weight_copies.append(start(region, region, CORE_WEIGHTS + 2 * number, other_core))
     corner_copies = []
     for number, spot_at in ((0, EAST), (1, WEST)):
         side_copies[number].wait_recv()
@@ -273,13 +299,6 @@
                     device,
                 )
             )
-    core_weight_copies = []
-    for number, step in enumerate((-1, 1, -far)):
-        weight_copies[number].wait_recv()
-        origin = (fsdp + step + FSDP) % FSDP
-        rows = pl.multiple_of(origin * own_cols + core * half_rows, half_rows)
-        region = wbuf.at[:, pl.ds(rows, half_rows), :]
-        core_weight_copies.append(start(region, region, CORE_WEIGHTS + number, other_core))
     grad_side_copies = []
     for number, spot_at, device in ((0, EAST, west), (1, WEST, east)):
         grad_side_copies.append(
@@ -291,8 +310,17 @@
             )
         )
 
+    for copy in tile_copies:
+        copy.wait_recv()
+    pair_rows = pl.ds(pl.multiple_of((2 - core) * TOK, TOK), TOK)
+    xt[:, pl.ds(TOK, TOK)] = xs[pair_rows, :].T
+    for number, origin in enumerate(origins):
+        for leg in range(2):
+            side_weight_copies[2 * number + leg].wait_recv()
+        region = weight_rows(origin, other_at, quarter)
+        core_weight_copies.append(start(region, region, CORE_WEIGHTS + 2 * number + 1, other_core))
     own_weight.wait()
-    for copy in tile_copies + core_weight_copies + corner_copies:
+    for copy in core_weight_copies + corner_copies:
         copy.wait_recv()
 
     @pl.loop(0, EXT // 256)
@@ -346,10 +374,10 @@
     ):
         stat_copies.append(start(src, stats_in.at[number], STATS + number, device))
 
-    parts = ((0, own_cols), (own_cols, 2 * own_cols))
+    parts = tuple((number * own_cols, own_cols) for number in (0, 2, 1))
     core_copies = []
-    x_copies = [[], []]
-    y_copies = [[], []]
+    x_copies = [[], [], []]
+    y_copies = [[], [], []]
     z_copies = []
 
     def share_with_core(part):
@@ -377,7 +405,7 @@
 
         def terms(owner):
             rows = pl.ds(pl.multiple_of(owner * TOK, TOK), TOK)
-            return dot(x2[:, rows], grads[:, cols], 0, 0)
+            return dot(xt[rows, :], grads[:, cols], 1, 0)
 
         for step in range(1, XS):
             gx_out[step - 1, :, cols] = terms(((x + step) % XS) * 2 + core).astype(BF16)
@@ -449,9 +477,6 @@
     weight_scale = 1.0 / math.sqrt(TOK * LATS * LONS)
     grads[own, pl.ds(0, own_cols)] = acc[0].astype(BF16)
     core_copies.append(share_with_core(0))
-    x2[own, :] = xs[own, :]
-    pair_rows = pl.ds(pl.multiple_of((2 - core) * TOK, TOK), TOK)
-    x2[pl.ds(TOK, TOK), :] = xs[pair_rows, :]
     for step in range(FSDP):
         gi_own[step] = input_terms((fsdp + step) % FSDP, (0,))
     send_x(0)
@@ -483,20 +508,28 @@
     def _(head):
         mine = lane == head
         key = jnp.where(mine, qkv[1, own, :], 0).astype(BF16)
-        value = jnp.where(mine, qkv[2, own, :], 0).astype(BF16)
         row_max = stat_rows[pl.ds(head, 1), :]
         inv_sum = stat_rows[pl.ds(own_heads + head, 1), :]
-        delta = stat_rows[pl.ds(2 * own_heads + head, 1), :]
         scores = dot(key, qkv[0], 1, 1) * scale + bias_b[...]
         prob = jnp.exp(jnp.minimum(scores - row_max, 0.0)) * inv_sum
+        probs[head] = prob
+        acc[2] = jnp.where(mine, dot(prob.astype(BF16), dos[...], 1, 0), acc[2])
+
+    grads[own, pl.ds(2 * own_cols, own_cols)] = acc[2].astype(BF16)
+    core_copies.append(share_with_core(1))
+
+    @pl.loop(0, own_heads)
+    def _(head):
+        mine = lane == head
+        value = jnp.where(mine, qkv[2, own, :], 0).astype(BF16)
+        delta = stat_rows[pl.ds(2 * own_heads + head, 1), :]
         grad_prob = dot(value, dos[...], 1, 1)
-        grad_score = (scale * (prob * (grad_prob - delta))).astype(BF16)
+        grad_score = (scale * (probs[head] * (grad_prob - delta))).astype(BF16)
         acc[1] = jnp.where(mine, dot(grad_score, qkv[0], 1, 0), acc[1])
-        acc[2] = jnp.where(mine, dot(prob.astype(BF16), dos[...], 1, 0), acc[2])
-
-    for number in (1, 2):
-        grads[own, pl.ds(number * own_cols, own_cols)] = acc[number].astype(BF16)
-    core_copies.append(share_with_core(1))
+
+    grads[own, pl.ds(own_cols, own_cols)] = acc[1].astype(BF16)
+    core_copies.append(share_with_core(2))
+    send_x(1)
 
     input_copies = []
     for step in range(1, FSDP):
@@ -505,19 +538,22 @@
         input_copies.append(
             start(gi_out.at[step - 1], gi_in.at[step - 1], INPUT_SUMS + step - 1, at(d_fsdp=peer))
         )
+    send_x(2)
+    send_y(0)
     gi_own[0] = gi_own[0] + input_terms(fsdp, (1, 2))
-    send_x(1)
-    send_y(0)
+    send_y(1)
+    send_z(0)
     for copy in input_copies:
         copy.wait_recv()
     grad_input[...] = (
         gi_own[0] + gi_in[0].astype(F32) + gi_in[1].astype(F32) + gi_in[2].astype(F32)
     ).astype(BF16)
-    send_z(0)
-    send_y(1)
+    send_y(2)
     send_z(1)
     finish(0)
+    send_z(2)
     finish(1)
+    finish(2)
 
     for copy in sent:
         copy.wait_send()
@@ -550,7 +586,8 @@
             pltpu.VMEM((8, 16, TOK), F32),
             pltpu.VMEM((16, EXT), F32),
             pltpu.VMEM((2 * TOK, total), BF16),
-            pltpu.VMEM((2 * TOK, width), BF16),
+            pltpu.VMEM((width, 2 * TOK), BF16),
+            pltpu.VMEM((own_cols // 64, TOK, EXT), F32),
             pltpu.VMEM((three, TOK, own_cols), F32),
             pltpu.VMEM((FSDP, TOK, own_cols), F32),
             pltpu.VMEM((FSDP - 1, TOK, own_cols), BF16),

time: 68.1 us -> 69.2 us (1.016)
  the two profiles are of different devices: /device:TPU:96 before, /device:TPU:1 now
where the time goes in v3:
time: 69.2 us; the launch traced here: 68.5 us
  Pallas kernels  65 us (94%)
  local copies, waits for them, and re-layouts  2.82 us (4%)
    pallas_call x1, Pallas kernels, shards(): pl.pallas_call(kernel, out_shape=(jax.ShapeDtypeStruct((TOK, own_cols), B...  65 us
    unnamed x2, local copies, waits for them, and re-layouts  2.82 us

profile of v3, /device:TPU:1, one launch (start us, length us, event | category | flops | bytes accessed | tf_op | source)
XLA Modules:
  0.0 68.5 jit_solution(11409293600385269088)
XLA Ops:
  0.6 65.0 %shard_map.50 = (bf16[128,256]{1,0:T(8,128)(2,1)}, f32[3,8,256]{2,1,0:T(8,128)}) custom-call(bf16[128,1024]{1,0:T(8,128)(2,1)} %bitcast.3, bf16[128,256]{1,0:T(8,128)(2,1)} %bitcast.5, bf16[3,256,1024]{2,1,0:T(8,128)(2,1)} %weight.1), custom_call_target="tpu_custom_call" | custom-call | tf_op jit(solution)/shard_map/pallas_call | solution.py:569
  65.7 1.5 %copy.7 = bf16[8,16,256]{2,1,0:T(8,128)(2,1)} copy(bf16[8,16,256]{2,1,0:T(8,128)(2,1)} %bitcast.4) | data formatting | bytes 131072
  67.1 1.3 %copy.8 = f32[3,8,256]{2,1,0:T(8,128)} copy(f32[3,8,256]{2,1,0:T(8,128)} %get-tuple-element.9) | data formatting | bytes 49152

commit v4 on v3

--- a/solution.py
+++ b/solution.py
@@ -29,8 +29,8 @@
 STATS = 31
 CORE_GRAD = 39
 INPUT_SUMS = 42
-SUM_X, SUM_Y, SUM_Z = 45, 54, 75
-COPIES = 78
+SUM_X, SUM_LON = 45, 54
+COPIES = 99
 
 
 def dot(a, b, ca, cb, precision=None):
@@ -88,7 +88,8 @@
     stat_rows,
     grads,
     xt,
-    probs,
+    scores_in,
+    grad_probs,
     acc,
     gi_own,
     gi_out,
@@ -96,11 +97,8 @@
     gx_out,
     gx_in,
     r1,
-    gy_out,
-    gy_in,
-    r2,
-    gz_out,
-    gz_in,
+    gl_out,
+    gl_in,
     send_sems,
     recv_sems,
     local_sems,
@@ -144,7 +142,10 @@
     def on_y(step):
         return at(d_lon=z_hi * YS + (y + step) % YS)
 
-    z_partner = at(d_lon=(1 - z_hi) * YS + y)
+    def on_lon(cross, step):
+        half = 1 - z_hi if cross else z_hi
+        return at(d_lon=half * YS + (y + step) % YS)
+
     corners = (
         at(d_lat=north_lat, d_lon=east_lon),
         at(d_lat=north_lat, d_lon=west_lon),
@@ -155,8 +156,8 @@
     partners += [on_z(step) for step in (1, -1, 2, -2)]
     partners += [at(d_fsdp=(fsdp + step) % FSDP) for step in range(1, FSDP)]
     partners += [on_x(step) for step in range(1, XS)]
-    partners += [on_y(step) for step in range(1, YS)]
-    partners += [z_partner]
+    lon_steps = [(1, step) for step in range(YS)] + [(0, step) for step in range(1, YS)]
+    partners += [on_lon(*step) for step in lon_steps]
 
     barrier = pltpu.get_barrier_semaphore()
     for partner in partners:
@@ -335,6 +336,19 @@
 
     stats[pl.ds(3 * own_heads, own_heads), :] = jnp.zeros((own_heads, TOK), F32)
 
+    grad_corner_copies = []
+    for number, spot_at in ((0, EAST), (1, WEST)):
+        grad_side_copies[number].wait_recv()
+        for leg, (device, block) in enumerate(((south, 4), (north, 5))):
+            grad_corner_copies.append(
+                start(
+                    dos.at[pl.ds(side + spot_at, SLAB)],
+                    dos.at[pl.ds(block * TOK + spot_at, SLAB)],
+                    GRADS + CORNERS + 2 * number + leg,
+                    device,
+                )
+            )
+
     @pl.loop(0, own_heads)
     def _(head):
         mine = lane == head
@@ -377,8 +391,7 @@
     parts = tuple((number * own_cols, own_cols) for number in (0, 2, 1))
     core_copies = []
     x_copies = [[], [], []]
-    y_copies = [[], [], []]
-    z_copies = []
+    lon_copies = [[], [], []]
 
     def share_with_core(part):
         cols = pl.ds(*parts[part])
@@ -419,80 +432,66 @@
             )
         r1[:, cols] = terms(lat)
 
-    def send_y(part):
-        cols = pl.ds(*parts[part])
+    def send_lon(part):
+        first, count = parts[part]
+        half = count // 2
+        cols = pl.ds(first, count)
+        folded = pl.ds(first // 2, half)
         for copy in x_copies[part]:
             copy.wait_recv()
         total = r1[:, cols]
         for number in range(XS - 1):
             total = total + gx_in[number, :, cols].astype(F32)
         r1[:, cols] = total
-        for step in range(1, YS):
-            gy_out[step - 1, :, cols] = both_halves((y + step) % YS, cols).astype(BF16)
-            y_copies[part].append(
+        for number, step in enumerate(lon_steps):
+            target = on_lon(*step)
+            rows = pl.ds(pl.multiple_of(target[1] * 8, 8), 8)
+            gl_out[number, :, folded] = jnp.concatenate(
+                [r1[rows, pl.ds(first, half)], r1[rows, pl.ds(first + half, half)]], axis=0
+            ).astype(BF16)
+            lon_copies[part].append(
                 start(
-                    gy_out.at[step - 1, :, cols],
-                    gy_in.at[step - 1, :, cols],
-                    SUM_Y + (YS - 1) * part + step - 1,
-                    on_y(step),
+                    gl_out.at[number, :, folded],
+                    gl_in.at[number, :, folded],
+                    SUM_LON + len(lon_steps) * part + number,
+                    target,
                 )
             )
-
-    def both_halves(owner, cols):
-        low = r1[pl.ds(pl.multiple_of(owner * 8, 8), 8), cols]
-        high = r1[pl.ds(pl.multiple_of(YS * 8 + owner * 8, 8), 8), cols]
-        return jnp.concatenate([low, high], axis=0)
-
-    def send_z(part):
-        first, count = parts[part]
-        cols = pl.ds(first, count)
-        half = count // 2
-        total = both_halves(y, cols)
-        for number, copy in enumerate(y_copies[part]):
-            copy.wait_recv()
-            total = total + gy_in[number, :, cols].astype(F32)
-        r2[:, cols] = total
-        rows = pl.ds(pl.multiple_of((1 - z_hi) * 8, 8), 8)
-        folded = pl.ds(first // 2, half)
-        gz_out[:, folded] = jnp.concatenate(
-            [r2[rows, pl.ds(first, half)], r2[rows, pl.ds(first + half, half)]], axis=0
-        ).astype(BF16)
-        z_copies.append(
-            start(gz_out.at[:, folded], gz_in.at[:, folded], SUM_Z + part, z_partner)
-        )
 
     def finish(part):
         first, count = parts[part]
         half = count // 2
-        z_copies[part].wait_recv()
-        other = gz_in[:, pl.ds(first // 2, half)].astype(F32)
-        own_rows = pl.ds(pl.multiple_of(z_hi * 8, 8), 8)
-        total = r2[own_rows, pl.ds(first, count)]
-        total = (total + jnp.concatenate([other[:8], other[8:]], axis=1)) * weight_scale
-        for number in range(count // own_cols):
-            grad_weight[first // own_cols + number] = total[
-                :, number * own_cols : (number + 1) * own_cols
-            ]
+        folded = pl.ds(first // 2, half)
+        rows = pl.ds(pl.multiple_of(lon * 8, 8), 8)
+        total = jnp.concatenate(
+            [r1[rows, pl.ds(first, half)], r1[rows, pl.ds(first + half, half)]], axis=0
+        )
+        for number in reversed(range(len(lon_steps))):
+            lon_copies[part][number].wait_recv()
+            total = total + gl_in[number, :, folded].astype(F32)
+        total = total * weight_scale
+        grad_weight[first // own_cols, :, pl.ds(0, half)] = total[:8]
+        grad_weight[first // own_cols, :, pl.ds(half, half)] = total[8:]
 
     weight_scale = 1.0 / math.sqrt(TOK * LATS * LONS)
     grads[own, pl.ds(0, own_cols)] = acc[0].astype(BF16)
     core_copies.append(share_with_core(0))
+
+    for copy in grad_tile_copies + grad_corner_copies:
+        copy.wait_recv()
+
+    @pl.loop(0, own_heads)
+    def _(head):
+        mine = lane == head
+        key = jnp.where(mine, qkv[1, own, :], 0).astype(BF16)
+        value = jnp.where(mine, qkv[2, own, :], 0).astype(BF16)
+        scores_in[head] = dot(key, qkv[0], 1, 1) * scale + bias_b[...]
+        grad_probs[head] = dot(value, dos[...], 1, 1)
+
     for step in range(FSDP):
         gi_own[step] = input_terms((fsdp + step) % FSDP, (0,))
     send_x(0)
-    grad_corner_copies = []
-    for number, spot_at in ((0, EAST), (1, WEST)):
-        grad_side_copies[number].wait_recv()
-        for leg, (device, block) in enumerate(((south, 4), (north, 5))):
-            grad_corner_copies.append(
-                start(
-                    dos.at[pl.ds(side + spot_at, SLAB)],
-                    dos.at[pl.ds(block * TOK + spot_at, SLAB)],
-                    GRADS + CORNERS + 2 * number + leg,
-                    device,
-                )
-            )
-    for copy in grad_tile_copies + grad_corner_copies + stat_copies:
+    for copy in stat_copies:
         copy.wait_recv()
     half_lane = lax.broadcasted_iota(jnp.int32, (16, TOK), 1) < 64
     stat_rows[:, pl.ds(0, TOK)] = stats[pl.ds(0, 16), :]
@@ -507,12 +506,10 @@
     @pl.loop(0, own_heads)
     def _(head):
         mine = lane == head
-        key = jnp.where(mine, qkv[1, own, :], 0).astype(BF16)
         row_max = stat_rows[pl.ds(head, 1), :]
         inv_sum = stat_rows[pl.ds(own_heads + head, 1), :]
-        scores = dot(key, qkv[0], 1, 1) * scale + bias_b[...]
-        prob = jnp.exp(jnp.minimum(scores - row_max, 0.0)) * inv_sum
-        probs[head] = prob
+        prob = jnp.exp(jnp.minimum(scores_in[head] - row_max, 0.0)) * inv_sum
+        scores_in[head] = prob
         acc[2] = jnp.where(mine, dot(prob.astype(BF16), dos[...], 1, 0), acc[2])
 
     grads[own, pl.ds(2 * own_cols, own_cols)] = acc[2].astype(BF16)
@@ -521,37 +518,33 @@
     @pl.loop(0, own_heads)
     def _(head):
         mine = lane == head
-        value = jnp.where(mine, qkv[2, own, :], 0).astype(BF16)
         delta = stat_rows[pl.ds(2 * own_heads + head, 1), :]
-        grad_prob = dot(value, dos[...], 1, 1)
-        grad_score = (scale * (probs[head] * (grad_prob - delta))).astype(BF16)
+        grad_score = (scale * (scores_in[head] * (grad_probs[head] - delta))).astype(BF16)
         acc[1] = jnp.where(mine, dot(grad_score, qkv[0], 1, 0), acc[1])
 
     grads[own, pl.ds(own_cols, own_cols)] = acc[1].astype(BF16)
     core_copies.append(share_with_core(2))
     send_x(1)
-
+    for step in range(FSDP):
+        gi_own[step] = gi_own[step] + input_terms((fsdp + step) % FSDP, (2,))
+    send_x(2)
     input_copies = []
     for step in range(1, FSDP):
         peer = (fsdp + step) % FSDP
-        gi_out[step - 1] = (gi_own[step] + input_terms(peer, (1, 2))).astype(BF16)
+        gi_out[step - 1] = (gi_own[step] + input_terms(peer, (1,))).astype(BF16)
         input_copies.append(
             start(gi_out.at[step - 1], gi_in.at[step - 1], INPUT_SUMS + step - 1, at(d_fsdp=peer))
         )
-    send_x(2)
-    send_y(0)
-    gi_own[0] = gi_own[0] + input_terms(fsdp, (1, 2))
-    send_y(1)
-    send_z(0)
+    gi_own[0] = gi_own[0] + input_terms(fsdp, (1,))
+    send_lon(0)
+    send_lon(1)
+    send_lon(2)
     for copy in input_copies:
         copy.wait_recv()
     grad_input[...] = (
         gi_own[0] + gi_in[0].astype(F32) + gi_in[1].astype(F32) + gi_in[2].astype(F32)
     ).astype(BF16)
-    send_y(2)
-    send_z(1)
     finish(0)
-    send_z(2)
     finish(1)
     finish(2)
 
@@ -588,6 +581,7 @@
             pltpu.VMEM((2 * TOK, total), BF16),
             pltpu.VMEM((width, 2 * TOK), BF16),
             pltpu.VMEM((own_cols // 64, TOK, EXT), F32),
+            pltpu.VMEM((own_cols // 64, TOK, EXT), F32),
             pltpu.VMEM((three, TOK, own_cols), F32),
             pltpu.VMEM((FSDP, TOK, own_cols), F32),
             pltpu.VMEM((FSDP - 1, TOK, own_cols), BF16),
@@ -595,11 +589,8 @@
             pltpu.VMEM((XS - 1, TOK, total), BF16),
             pltpu.VMEM((XS - 1, TOK, total), BF16),
             pltpu.VMEM((TOK, total), F32),
-            pltpu.VMEM((YS - 1, 16, total), BF16),
-            pltpu.VMEM((YS - 1, 16, total), BF16),
-            pltpu.VMEM((16, total), F32),
-            pltpu.VMEM((16, total // 2), BF16),
-            pltpu.VMEM((16, total // 2), BF16),
+            pltpu.VMEM((LONS - 1, 16, total // 2), BF16),
+            pltpu.VMEM((LONS - 1, 16, total // 2), BF16),
             pltpu.SemaphoreType.DMA((COPIES,)),
             pltpu.SemaphoreType.DMA((COPIES,)),
             pltpu.SemaphoreType.DMA((3,)),

time: 69.2 us -> 67.6 us (0.977)
  Pallas kernels: 65 us -> 63.8 us
    pallas_call x1, Pallas kernels: 65 us -> 63.8 us  [shards(): pl.pallas_call(kernel, out_shape=(jax.ShapeDtypeStruct((TOK, own_cols), B...]
where the time goes in v4:
time: 67.6 us; the launch traced here: 67.2 us
  Pallas kernels  63.8 us (94%)
  local copies, waits for them, and re-layouts  2.82 us (4%)
    pallas_call x1, Pallas kernels, shards(): pl.pallas_call(kernel, out_shape=(jax.ShapeDtypeStruct((TOK, own_cols), B...  63.8 us
    unnamed x2, local copies, waits for them, and re-layouts  2.82 us

profile of v4, /device:TPU:1, one launch (start us, length us, event | category | flops | bytes accessed | tf_op | source)
XLA Modules:
  0.0 67.2 jit_solution(11093012023842260181)
XLA Ops:
  0.6 63.8 %shard_map.50 = (bf16[128,256]{1,0:T(8,128)(2,1)}, f32[3,8,256]{2,1,0:T(8,128)}) custom-call(bf16[128,1024]{1,0:T(8,128)(2,1)} %bitcast.3, bf16[128,256]{1,0:T(8,128)(2,1)} %bitcast.5, bf16[3,256,1024]{2,1,0:T(8,128)(2,1)} %weight.1), custom_call_target="tpu_custom_call" | custom-call | tf_op jit(solution)/shard_map/pallas_call | solution.py:562
  64.4 1.5 %copy.7 = bf16[8,16,256]{2,1,0:T(8,128)(2,1)} copy(bf16[8,16,256]{2,1,0:T(8,128)(2,1)} %bitcast.4) | data formatting | bytes 131072
  65.9 1.3 %copy.8 = f32[3,8,256]{2,1,0:T(8,128)} copy(f32[3,8,256]{2,1,0:T(8,128)} %get-tuple-element.9) | data formatting | bytes 49152

commit v5 on v4

--- a/solution.py
+++ b/solution.py
@@ -88,6 +88,8 @@
     stat_rows,
     grads,
     xt,
+    probs,
+    own_grad_probs,
     scores_in,
     grad_probs,
     acc,
@@ -152,7 +154,7 @@
         at(d_lat=south_lat, d_lon=east_lon),
         at(d_lat=south_lat, d_lon=west_lon),
     )
-    partners = [south, north, east, west, east_copy, west_copy, *corners]
+    partners = [*corners, east_copy, west_copy, south, north]
     partners += [on_z(step) for step in (1, -1, 2, -2)]
     partners += [at(d_fsdp=(fsdp + step) % FSDP) for step in range(1, FSDP)]
     partners += [on_x(step) for step in range(1, XS)]
@@ -336,20 +338,7 @@
 
     stats[pl.ds(3 * own_heads, own_heads), :] = jnp.zeros((own_heads, TOK), F32)
 
-    grad_corner_copies = []
-    for number, spot_at in ((0, EAST), (1, WEST)):
-        grad_side_copies[number].wait_recv()
-        for leg, (device, block) in enumerate(((south, 4), (north, 5))):
-            grad_corner_copies.append(
-                start(
-                    dos.at[pl.ds(side + spot_at, SLAB)],
-                    dos.at[pl.ds(block * TOK + spot_at, SLAB)],
-                    GRADS + CORNERS + 2 * number + leg,
-                    device,
-                )
-            )
-
-    @pl.loop(0, own_heads)
+    @pl.loop(0, own_heads, unroll=True)
     def _(head):
         mine = lane == head
         query = jnp.where(mine, qkv[0, own, :], 0).astype(BF16)
@@ -361,9 +350,8 @@
         prob = prob * inv_sum
         grad_prob = dot(qkv[2], cotangent, 1, 1)
         delta = jnp.sum(prob * grad_prob, axis=0, keepdims=True)
-        grad_score = (scale * (prob * (grad_prob - delta))).astype(BF16)
-        part = dot(grad_score, qkv[1], 0, 0)
-        acc[0] = jnp.where(mine, part, acc[0])
+        probs[head] = prob
+        own_grad_probs[head] = grad_prob
         stats[pl.ds(head, 1), :] = row_max
         stats[pl.ds(own_heads + head, 1), :] = inv_sum
         stats[pl.ds(2 * own_heads + head, 1), :] = delta
@@ -387,6 +375,19 @@
         )
     ):
         stat_copies.append(start(src, stats_in.at[number], STATS + number, device))
+
+    grad_corner_copies = []
+    for number, spot_at in ((0, EAST), (1, WEST)):
+        grad_side_copies[number].wait_recv()
+        for leg, (device, block) in enumerate(((south, 4), (north, 5))):
+            grad_corner_copies.append(
+                start(
+                    dos.at[pl.ds(side + spot_at, SLAB)],
+                    dos.at[pl.ds(block * TOK + spot_at, SLAB)],
+                    GRADS + CORNERS + 2 * number + leg,
+                    device,
+                )
+            )
 
     parts = tuple((number * own_cols, own_cols) for number in (0, 2, 1))
     core_copies = []
@@ -473,14 +474,24 @@
         grad_weight[first // own_cols, :, pl.ds(0, half)] = total[:8]
         grad_weight[first // own_cols, :, pl.ds(half, half)] = total[8:]
 
+    @pl.loop(0, own_heads, unroll=True)
+    def _(head):
+        mine = lane == head
+        delta = stats[pl.ds(2 * own_heads + head, 1), :]
+        grad_score = (scale * (probs[head] * (own_grad_probs[head] - delta))).astype(BF16)
+        acc[0] = jnp.where(mine, dot(grad_score, qkv[1], 0, 0), acc[0])
+
     weight_scale = 1.0 / math.sqrt(TOK * LATS * LONS)
     grads[own, pl.ds(0, own_cols)] = acc[0].astype(BF16)
     core_copies.append(share_with_core(0))
 
+    for step in range(FSDP):
+        gi_own[step] = input_terms((fsdp + step) % FSDP, (0,))
+    send_x(0)
     for copy in grad_tile_copies + grad_corner_copies:
         copy.wait_recv()
 
-    @pl.loop(0, own_heads)
+    @pl.loop(0, own_heads, unroll=True)
     def _(head):
         mine = lane == head
         key = jnp.where(mine, qkv[1, own, :], 0).astype(BF16)
@@ -488,9 +499,6 @@
         scores_in[head] = dot(key, qkv[0], 1, 1) * scale + bias_b[...]
         grad_probs[head] = dot(value, dos[...], 1, 1)
 
-    for step in range(FSDP):
-        gi_own[step] = input_terms((fsdp + step) % FSDP, (0,))
-    send_x(0)
     for copy in stat_copies:
         copy.wait_recv()
     half_lane = lax.broadcasted_iota(jnp.int32, (16, TOK), 1) < 64
@@ -503,7 +511,7 @@
             half_lane, stats_in[first], stats_in[first + 1]
         )
 
-    @pl.loop(0, own_heads)
+    @pl.loop(0, own_heads, unroll=True)
     def _(head):
         mine = lane == head
         row_max = stat_rows[pl.ds(head, 1), :]
@@ -515,7 +523,7 @@
     grads[own, pl.ds(2 * own_cols, own_cols)] = acc[2].astype(BF16)
     core_copies.append(share_with_core(1))
 
-    @pl.loop(0, own_heads)
+    @pl.loop(0, own_heads, unroll=True)
     def _(head):
         mine = lane == head
         delta = stat_rows[pl.ds(2 * own_heads + head, 1), :]
@@ -538,13 +546,13 @@
     gi_own[0] = gi_own[0] + input_terms(fsdp, (1,))
     send_lon(0)
     send_lon(1)
+    finish(0)
     send_lon(2)
     for copy in input_copies:
         copy.wait_recv()
     grad_input[...] = (
         gi_own[0] + gi_in[0].astype(F32) + gi_in[1].astype(F32) + gi_in[2].astype(F32)
     ).astype(BF16)
-    finish(0)
     finish(1)
     finish(2)
 
@@ -580,6 +588,8 @@
             pltpu.VMEM((16, EXT), F32),
             pltpu.VMEM((2 * TOK, total), BF16),
             pltpu.VMEM((width, 2 * TOK), BF16),
+            pltpu.VMEM((own_cols // 64, EXT, TOK), F32),
+            pltpu.VMEM((own_cols // 64, EXT, TOK), F32),
             pltpu.VMEM((own_cols // 64, TOK, EXT), F32),
             pltpu.VMEM((own_cols // 64, TOK, EXT), F32),
             pltpu.VMEM((three, TOK, own_cols), F32),

time: 67.6 us -> 68.5 us (1.013)
  Pallas kernels: 63.8 us -> 64.9 us
    pallas_call x1, Pallas kernels: 63.8 us -> 64.9 us  [shards(): pl.pallas_call(kernel, out_shape=(jax.ShapeDtypeStruct((TOK, own_cols), B...]
where the time goes in v5:
time: 68.5 us; the launch traced here: 68.3 us
  Pallas kernels  64.9 us (95%)
  local copies, waits for them, and re-layouts  2.82 us (4%)
    pallas_call x1, Pallas kernels, shards(): pl.pallas_call(kernel, out_shape=(jax.ShapeDtypeStruct((TOK, own_cols), B...  64.9 us
    unnamed x2, local copies, waits for them, and re-layouts  2.82 us

profile of v5, /device:TPU:1, one launch (start us, length us, event | category | flops | bytes accessed | tf_op | source)
XLA Modules:
  0.0 68.3 jit_solution(14039084435966369670)
XLA Ops:
  0.6 64.9 %shard_map.50 = (bf16[128,256]{1,0:T(8,128)(2,1)}, f32[3,8,256]{2,1,0:T(8,128)}) custom-call(bf16[128,1024]{1,0:T(8,128)(2,1)} %bitcast.3, bf16[128,256]{1,0:T(8,128)(2,1)} %bitcast.5, bf16[3,256,1024]{2,1,0:T(8,128)(2,1)} %weight.1), custom_call_target="tpu_custom_call" | custom-call | tf_op jit(solution)/shard_map/pallas_call | solution.py:570
  65.5 1.5 %copy.7 = bf16[8,16,256]{2,1,0:T(8,128)(2,1)} copy(bf16[8,16,256]{2,1,0:T(8,128)(2,1)} %bitcast.4) | data formatting | bytes 131072
  67.0 1.3 %copy.8 = f32[3,8,256]{2,1,0:T(8,128)} copy(f32[3,8,256]{2,1,0:T(8,128)} %get-tuple-element.9) | data formatting | bytes 49152

commit v6 on v5

--- a/solution.py
+++ b/solution.py
@@ -30,7 +30,7 @@
 CORE_GRAD = 39
 INPUT_SUMS = 42
 SUM_X, SUM_LON = 45, 54
-COPIES = 99
+COPIES = 84
 
 
 def dot(a, b, ca, cb, precision=None):
@@ -392,7 +392,8 @@
     parts = tuple((number * own_cols, own_cols) for number in (0, 2, 1))
     core_copies = []
     x_copies = [[], [], []]
-    lon_copies = [[], [], []]
+    groups = ((0, 1), (2,))
+    lon_copies = [[], []]
 
     def share_with_core(part):
         cols = pl.ds(*parts[part])
@@ -433,42 +434,47 @@
             )
         r1[:, cols] = terms(lat)
 
-    def send_lon(part):
-        first, count = parts[part]
-        half = count // 2
-        cols = pl.ds(first, count)
-        folded = pl.ds(first // 2, half)
-        for copy in x_copies[part]:
-            copy.wait_recv()
-        total = r1[:, cols]
-        for number in range(XS - 1):
-            total = total + gx_in[number, :, cols].astype(F32)
-        r1[:, cols] = total
+    def send_lon(group):
+        for part in groups[group]:
+            cols = pl.ds(*parts[part])
+            for copy in x_copies[part]:
+                copy.wait_recv()
+            total = r1[:, cols]
+            for number in range(XS - 1):
+                total = total + gx_in[number, :, cols].astype(F32)
+            r1[:, cols] = total
+        half = own_cols // 2
+        sent_cols = pl.ds(groups[group][0] * half, len(groups[group]) * half)
         for number, step in enumerate(lon_steps):
             target = on_lon(*step)
             rows = pl.ds(pl.multiple_of(target[1] * 8, 8), 8)
-            gl_out[number, :, folded] = jnp.concatenate(
-                [r1[rows, pl.ds(first, half)], r1[rows, pl.ds(first + half, half)]], axis=0
-            ).astype(BF16)
-            lon_copies[part].append(
+            for part in groups[group]:
+                first = parts[part][0]
+                gl_out[number, :, pl.ds(part * half, half)] = jnp.concatenate(
+                    [r1[rows, pl.ds(first, half)], r1[rows, pl.ds(first + half, half)]], axis=0
+                ).astype(BF16)
+            lon_copies[group].append(
                 start(
-                    gl_out.at[number, :, folded],
-                    gl_in.at[number, :, folded],
-                    SUM_LON + len(lon_steps) * part + number,
+                    gl_out.at[number, :, sent_cols],
+                    gl_in.at[number, :, sent_cols],
+                    SUM_LON + len(lon_steps) * group + number,
                     target,
                 )
             )
+
+    def arrive(group):
+        for copy in reversed(lon_copies[group]):
+            copy.wait_recv()
 
     def finish(part):
         first, count = parts[part]
         half = count // 2
-        folded = pl.ds(first // 2, half)
+        folded = pl.ds(part * half, half)
         rows = pl.ds(pl.multiple_of(lon * 8, 8), 8)
         total = jnp.concatenate(
             [r1[rows, pl.ds(first, half)], r1[rows, pl.ds(first + half, half)]], axis=0
         )
-        for number in reversed(range(len(lon_steps))):
-            lon_copies[part][number].wait_recv()
+        for number in range(len(lon_steps)):
             total = total + gl_in[number, :, folded].astype(F32)
         total = total * weight_scale
         grad_weight[first // own_cols, :, pl.ds(0, half)] = total[:8]
@@ -546,14 +552,15 @@
     gi_own[0] = gi_own[0] + input_terms(fsdp, (1,))
     send_lon(0)
     send_lon(1)
-    finish(0)
-    send_lon(2)
     for copy in input_copies:
         copy.wait_recv()
     grad_input[...] = (
         gi_own[0] + gi_in[0].astype(F32) + gi_in[1].astype(F32) + gi_in[2].astype(F32)
     ).astype(BF16)
+    arrive(0)
+    finish(0)
     finish(1)
+    arrive(1)
     finish(2)
 
     for copy in sent:

time: 68.5 us -> 63.5 us (0.927)
  Pallas kernels: 64.9 us -> 59.8 us
    pallas_call x1, Pallas kernels: 64.9 us -> 59.8 us  [shards(): pl.pallas_call(kernel, out_shape=(jax.ShapeDtypeStruct((TOK, own_cols), B...]
where the time goes in v6:
time: 63.5 us; the launch traced here: 63.3 us
  Pallas kernels  59.8 us (94%)
  local copies, waits for them, and re-layouts  2.82 us (4%)
  between operations  0.64 us (1%)
    pallas_call x1, Pallas kernels, shards(): pl.pallas_call(kernel, out_shape=(jax.ShapeDtypeStruct((TOK, own_cols), B...  59.8 us
    unnamed x2, local copies, waits for them, and re-layouts  2.82 us

profile of v6, /device:TPU:1, one launch (start us, length us, event | category | flops | bytes accessed | tf_op | source)
XLA Modules:
  0.0 63.3 jit_solution(11916325972445787321)
XLA Ops:
  0.6 59.8 %shard_map.50 = (bf16[128,256]{1,0:T(8,128)(2,1)}, f32[3,8,256]{2,1,0:T(8,128)}) custom-call(bf16[128,1024]{1,0:T(8,128)(2,1)} %bitcast.3, bf16[128,256]{1,0:T(8,128)(2,1)} %bitcast.5, bf16[3,256,1024]{2,1,0:T(8,128)(2,1)} %weight.1), custom_call_target="tpu_custom_call" | custom-call | tf_op jit(solution)/shard_map/pallas_call | solution.py:577
  60.5 1.5 %copy.7 = bf16[8,16,256]{2,1,0:T(8,128)(2,1)} copy(bf16[8,16,256]{2,1,0:T(8,128)(2,1)} %bitcast.4) | data formatting | bytes 131072
  61.9 1.3 %copy.8 = f32[3,8,256]{2,1,0:T(8,128)} copy(f32[3,8,256]{2,1,0:T(8,128)} %get-tuple-element.9) | data formatting | bytes 49152

commit v7 on v6

--- a/solution.py
+++ b/solution.py
@@ -30,7 +30,7 @@
 CORE_GRAD = 39
 INPUT_SUMS = 42
 SUM_X, SUM_LON = 45, 54
-COPIES = 84
+COPIES = 69
 
 
 def dot(a, b, ca, cb, precision=None):
@@ -392,8 +392,8 @@
     parts = tuple((number * own_cols, own_cols) for number in (0, 2, 1))
     core_copies = []
     x_copies = [[], [], []]
-    groups = ((0, 1), (2,))
-    lon_copies = [[], []]
+    groups = ((0, 1, 2),)
+    lon_copies = [[]]
 
     def share_with_core(part):
         cols = pl.ds(*parts[part])
@@ -551,7 +551,6 @@
         )
     gi_own[0] = gi_own[0] + input_terms(fsdp, (1,))
     send_lon(0)
-    send_lon(1)
     for copy in input_copies:
         copy.wait_recv()
     grad_input[...] = (
@@ -560,7 +559,6 @@
     arrive(0)
     finish(0)
     finish(1)
-    arrive(1)
     finish(2)
 
     for copy in sent:

time: 63.5 us -> 64.2 us (1.011); the launches traced: 63.3 us -> 63.3 us
  no operation moved by 1% of the time
where the time goes in v7:
time: 64.2 us; the launch traced here: 63.3 us
  Pallas kernels  59.8 us (93%)
  local copies, waits for them, and re-layouts  2.82 us (4%)
    pallas_call x1, Pallas kernels, shards(): pl.pallas_call(kernel, out_shape=(jax.ShapeDtypeStruct((TOK, own_cols), B...  59.8 us
    unnamed x2, local copies, waits for them, and re-layouts  2.82 us

profile of v7, /device:TPU:1, one launch (start us, length us, event | category | flops | bytes accessed | tf_op | source)
XLA Modules:
  0.0 63.3 jit_solution(16501197262023554011)
XLA Ops:
  0.6 59.8 %shard_map.50 = (bf16[128,256]{1,0:T(8,128)(2,1)}, f32[3,8,256]{2,1,0:T(8,128)}) custom-call(bf16[128,1024]{1,0:T(8,128)(2,1)} %bitcast.3, bf16[128,256]{1,0:T(8,128)(2,1)} %bitcast.5, bf16[3,256,1024]{2,1,0:T(8,128)(2,1)} %weight.1), custom_call_target="tpu_custom_call" | custom-call | tf_op jit(solution)/shard_map/pallas_call | solution.py:575
  60.5 1.5 %copy.7 = bf16[8,16,256]{2,1,0:T(8,128)(2,1)} copy(bf16[8,16,256]{2,1,0:T(8,128)(2,1)} %bitcast.4) | data formatting | bytes 131072
  61.9 1.3 %copy.8 = f32[3,8,256]{2,1,0:T(8,128)} copy(f32[3,8,256]{2,1,0:T(8,128)} %get-tuple-element.9) | data formatting | bytes 49152
